TPU v7x, 32 devices: a whole 2x2x4 slice. The times are simulated.
32 devices in a mesh: tm: 8 (over y, x, core), space: 4 (over z).
Axes of the slice: x: 2, y: 2, z: 4, core: 2. Of those that a mesh axis runs over, the one named last changes fastest.
Arguments:
- state: float32 [64, 96, 128], P('tm', 'space'), may hold values from -6 to 6
- forcing: float32 [64, 96, 128], P('tm', 'space'), may hold values from -6 to 6
- initial: float32 [96, 128], P('space'), may hold values from -6 to 6
- blocks: bfloat16 [5, 96, 128, 128], P(None, 'space'), may hold values from -0.25 to 0.25
- precond: bfloat16 [96, 128, 128], P('space'), may hold values from -0.5 to 0.5
- couple: int32 [96, 5], P('space'), may hold values from -2 to 2
Outputs:
- corrected: float32 [64, 96, 128], P('tm', 'space')
Inputs may be any that keep to these rules, and one draw needn't show every extreme that they name: Row j, slot s couples to block row j + couple[j, s].
All inputs are finite; a program needn't handle non-finite values.
Results may differ from a plain program's by a relative error of at most 0.002.
Values may be sent and summed in bfloat16 or wider, within the bound.
A program may use at most 64 MiB of HBM per device.

v0:
```python
import math

import jax
import jax.numpy as jnp
from jax import lax
from jax.sharding import PartitionSpec as P

SWEEPS = 2


alpha_rate = 0.5
time_step = 0.5
relaxation = 0.7


def from_behind(block, axis, distance):
    devices = range(lax.axis_size(axis))
    route = [(i - distance, i) for i in devices if i - distance in devices]
    return lax.ppermute(block, axis, route)


def extended(block, sides, width):
    for axis, dim in sides:
        count = lax.axis_size(axis)
        forward = [(i, i + 1) for i in range(count - 1)]
        backward = [(target, source) for source, target in forward]
        low = lax.ppermute(
            lax.slice_in_dim(block, block.shape[dim] - width, None, axis=dim), axis, forward
        )
        high = lax.ppermute(lax.slice_in_dim(block, 0, width, axis=dim), axis, backward)
        block = jnp.concatenate([low, block, high], axis=dim)
    return block


def from_partner(block, axis, stride):
    count = lax.axis_size(axis)
    route = []
    for low in range(count):
        high = low | 1 << stride
        if high != low and high < count:
            route += [(low, high), (high, low)]
    return lax.ppermute(block, axis, route)


def apply_padded(padded, blocks, couple):
    width = padded.shape[1] - 4
    total = None
    for column in range(5):
        chosen = padded[:, 2 : 2 + width]
        for offset in range(-2, 3):
            picked = (couple[:, column] == offset)[None, :, None]
            chosen = jnp.where(picked, padded[:, 2 + offset : 2 + offset + width], chosen)
        term = jnp.einsum(
            "fbj,bij->fbi", chosen, blocks[column], preferred_element_type=jnp.float32
        )
        total = term if total is None else total + term
    return total


def on_device(state, forcing, initial, blocks, precond, couple):
    local_steps = state.shape[0]
    devices_tm = lax.axis_size("tm")
    position = lax.axis_index("tm")
    total_steps = local_steps * devices_tm
    level_count = devices_tm.bit_length() - 1
    highest = lax.Precision.HIGHEST
    last_step = from_behind(state[-1:], "tm", 1)
    first_prev = jnp.where(position == 0, initial[None], last_step)
    previous = jnp.concatenate([first_prev, state[:-1]], 0)
    squares = (0.5 * state * state).astype(jnp.bfloat16)
    padded = extended(squares, (("space", 1),), 2)
    flux = apply_padded(padded, blocks, couple)
    residual = forcing - state + previous - time_step * flux
    steps_global = position * local_steps + jnp.arange(local_steps, dtype=jnp.int32)
    log_rate = math.log(alpha_rate) / total_steps
    scaled = residual * jnp.exp(steps_global.astype(jnp.float32) * log_rate)[:, None, None]
    cur_re = scaled
    cur_im = jnp.zeros_like(scaled)
    for level in range(level_count):
        bit_number = level_count - 1 - level
        half = 1 << bit_number
        other = from_partner(jnp.stack([cur_re, cur_im]), "tm", bit_number)
        upper = position >> bit_number & 1 == 1
        angle = -2.0 * math.pi * (position % half).astype(jnp.float32) / (2 * half)
        tw_re = jnp.cos(angle)
        tw_im = jnp.sin(angle)
        diff_re = other[0] - cur_re
        diff_im = other[1] - cur_im
        new_re = jnp.where(upper, diff_re * tw_re - diff_im * tw_im, cur_re + other[0])
        new_im = jnp.where(upper, diff_re * tw_im + diff_im * tw_re, cur_im + other[1])
        cur_re, cur_im = (new_re, new_im)
    freq_base = jnp.zeros((), jnp.int32)
    for level in range(level_count):
        freq_base = freq_base + (position >> level & 1) * (1 << level_count - 1 - level)
    part_re, part_im = (cur_re, cur_im)
    local_index = jnp.arange(local_steps, dtype=jnp.int32)
    freq = freq_base + devices_tm * local_index
    product = freq[:, None] * local_index[None, :] % total_steps
    angle_table = 2.0 * math.pi * product.astype(jnp.float32) / total_steps
    table_re = jnp.cos(angle_table)
    table_im = -jnp.sin(angle_table)
    spec_re = jnp.einsum("qm,mbc->qbc", table_re, part_re, precision=highest) - jnp.einsum(
        "qm,mbc->qbc", table_im, part_im, precision=highest
    )
    spec_im = jnp.einsum("qm,mbc->qbc", table_re, part_im, precision=highest) + jnp.einsum(
        "qm,mbc->qbc", table_im, part_re, precision=highest
    )
    theta = 2.0 * math.pi * freq.astype(jnp.float32) / total_steps
    rate = math.exp(log_rate)
    lam_re = (1.0 - rate * jnp.cos(theta))[:, None, None]
    lam_im = (rate * jnp.sin(theta))[:, None, None]
    denom = (1.0 + lam_re) ** 2 + lam_im**2
    coef_re = (1.0 + lam_re) / denom
    coef_im = -lam_im / denom
    sol_re = None
    sol_im = None
    for sweep in range(SWEEPS):
        if sweep == 0:
            res_re, res_im = (spec_re, spec_im)
        else:
            stacked = jnp.concatenate([sol_re, sol_im], 0).astype(jnp.bfloat16)
            padded_sol = extended(stacked, (("space", 1),), 2)
            applied = apply_padded(padded_sol, blocks, couple)
            res_re = (
                spec_re - (lam_re * sol_re - lam_im * sol_im) - time_step * applied[:local_steps]
            )
            res_im = (
                spec_im - (lam_re * sol_im + lam_im * sol_re) - time_step * applied[local_steps:]
            )
        rounded = jnp.concatenate([res_re, res_im], 0).astype(jnp.bfloat16)
        gres = jnp.einsum("fbj,bij->fbi", rounded, precond, preferred_element_type=jnp.float32)
        g_re = gres[:local_steps]
        g_im = gres[local_steps:]
        step_re = relaxation * (coef_re * g_re - coef_im * g_im)
        step_im = relaxation * (coef_re * g_im + coef_im * g_re)
        if sweep == 0:
            sol_re, sol_im = (step_re, step_im)
        else:
            sol_re = sol_re + step_re
            sol_im = sol_im + step_im
    back_re = (
        jnp.einsum("qm,qbc->mbc", table_re, sol_re, precision=highest)
        + jnp.einsum("qm,qbc->mbc", table_im, sol_im, precision=highest)
    ) / local_steps
    back_im = (
        jnp.einsum("qm,qbc->mbc", table_re, sol_im, precision=highest)
        - jnp.einsum("qm,qbc->mbc", table_im, sol_re, precision=highest)
    ) / local_steps
    cur_re, cur_im = (back_re, back_im)
    for bit_number in range(level_count):
        half = 1 << bit_number
        other = from_partner(jnp.stack([cur_re, cur_im]), "tm", bit_number)
        upper = position >> bit_number & 1 == 1
        angle = -2.0 * math.pi * (position % half).astype(jnp.float32) / (2 * half)
        conj_re = jnp.cos(angle)
        conj_im = -jnp.sin(angle)
        other_tw_re = other[0] * conj_re - other[1] * conj_im
        other_tw_im = other[0] * conj_im + other[1] * conj_re
        mine_tw_re = cur_re * conj_re - cur_im * conj_im
        mine_tw_im = cur_re * conj_im + cur_im * conj_re
        new_re = jnp.where(upper, 0.5 * (other[0] - mine_tw_re), 0.5 * (cur_re + other_tw_re))
        new_im = jnp.where(upper, 0.5 * (other[1] - mine_tw_im), 0.5 * (cur_im + other_tw_im))
        cur_re, cur_im = (new_re, new_im)
    change = cur_re * jnp.exp(-steps_global.astype(jnp.float32) * log_rate)[:, None, None]
    return state + change


def solution(mesh):
    placed = (
        P("tm", "space", None),
        P("tm", "space", None),
        P("space", None),
        P(None, "space", None, None),
        P("space", None, None),
        P("space", None),
    )
    return jax.shard_map(
        on_device, mesh=mesh, in_specs=placed, out_specs=P("tm", "space", None), check_vma=False
    )
```

profile of v0, /device:TPU:0, one launch (start us, length us, event | category | flops | bytes accessed | tf_op | source)
XLA Modules:
  0.0 68.1 jit_solution(299057052072444461)
XLA Ops:
  0.0 0.8 %slice.92 = f32[1,24,128]{2,1,0:T(8,128)S(1)} slice(f32[8,24,128]{2,1,0:T(8,128)} %param.6), slice={[7:8], [0:24], [0:128]} | slice | bytes 24576 | tf_op jit(solution)/shard_map/slice | solution.py:67
  0.8 2.3 %collective-permute-start = (f32[1,24,128]{2,0,1:T(1,128)S(1)}, f32[1,24,128]{2,0,1:T(1,128)S(1)}, u32[]{:S(2)}, u32[]{:S(2)}) collective-permute-start(f32[1,24,128]{2,0,1:T(1,128)S(1)} %bitcast.248), channel_id=1, source_target_pairs={{0,4},{4,8},{8,12},{12,16},{16,20},{20,24},{24,28},{1,5},{5,9},{9,... | collective-permute-start | bytes 36872 | tf_op jit(solution)/shard_map/ppermute | solution.py:19
  3.2 0.9 %fusion.25 = bf16[8,24,128]{2,0,1:T(8,128)(2,1)S(1)} fusion(f32[8,24,128]{2,1,0:T(8,128)} %param.6), kind=kLoop, calls=%fused_computation.52 | loop fusion | flops 73728 | bytes 147456 | tf_op jit(solution)/shard_map/convert_element_type | solution.py:70
  4.1 4.3 %collective-permute-start.2 = (bf16[8,2,128]{2,0,1:T(8,128)(2,1)S(1)}, bf16[8,2,128]{2,0,1:T(8,128)(2,1)S(1)}, u32[]{:S(2)}, u32[]{:S(2)}) collective-permute-start(bf16[8,2,128]{2,0,1:T(8,128)(2,1)S(1)} %get-tuple-element.31), channel_id=1, source_target_pairs={{0,1},{1,2},{2,3},{4,5},{5,6},{6,7},{8,9},{9,10},{10,11},{12,13},{... | collective-permute-start | bytes 12296 | tf_op jit(solution)/shard_map/ppermute | solution.py:27
  8.4 1.3 %collective-permute-start.1 = (bf16[8,2,128]{2,0,1:T(8,128)(2,1)S(1)}, bf16[8,2,128]{2,0,1:T(8,128)(2,1)S(1)}, u32[]{:S(2)}, u32[]{:S(2)}) collective-permute-start(bf16[8,2,128]{2,0,1:T(8,128)(2,1)S(1)} %get-tuple-element.32), channel_id=1, source_target_pairs={{1,0},{2,1},{3,2},{5,4},{6,5},{7,6},{9,8},{10,9},{11,10},{13,12},{... | collective-permute-start | bytes 12296 | tf_op jit(solution)/shard_map/ppermute | solution.py:30
  9.7 0.9 %compare_bitcast_fusion.1 = (pred[24]{0:T(512)(128)(4,1)S(1)}, pred[24]{0:T(512)(128)(4,1)S(1)}, pred[24]{0:T(512)(128)(4,1)S(1)}, pred[24]{0:T(512)(128)(4,1)S(...) fusion(s32[24,5]{0,1:T(8,128)} %param.11), kind=kLoop, calls=%fused_computation.271 | loop fusion | flops 144 | bytes 624 | tf_op jit(solution)/shard_map/eq | solution.py:51
  10.6 0.9 %compare_bitcast_fusion.4 = (pred[24]{0:T(512)(128)(4,1)S(1)}, pred[24]{0:T(512)(128)(4,1)S(1)}, pred[24]{0:T(512)(128)(4,1)S(1)}, pred[24]{0:T(512)(128)(4,1)S(...) fusion(s32[24,5]{0,1:T(8,128)} %param.11), kind=kLoop, calls=%fused_computation.274 | loop fusion | flops 456 | bytes 936 | tf_op jit(solution)/shard_map/eq | solution.py:51
  11.5 0.9 %slice.134 = f32[7,24,128]{2,1,0:T(8,128)S(1)} slice(f32[8,24,128]{2,1,0:T(8,128)} %param.6), slice={[0:7], [0:24], [0:128]} | slice | bytes 172032 | tf_op jit(solution)/shard_map/slice | solution.py:69
  12.4 1.5 %collective-permute-done.1 = bf16[8,2,128]{2,0,1:T(8,128)(2,1)S(1)} collective-permute-done((bf16[8,2,128]{2,0,1:T(8,128)(2,1)S(1)}, bf16[8,2,128]{2,0,1:T(8,128)(2,1)S(1)}, u32[]{:S(2)}, u32[]{:S(2)}) %collective-permute-start.1) | collective-permute-done | bytes 4128 | tf_op jit(solution)/shard_map/ppermute | solution.py:30
  13.9 1.7 %fusion.11 = f32[24,8,128]{2,1,0:T(8,128)S(1)} fusion(bf16[5,24,128,128]{3,2,1,0:T(8,128)(2,1)} %param.9, bf16[8,24,128]{2,0,1:T(8,128)(2,1)S(1)} %get-tuple-element.30, bf16[8,24,128]{2,0,1:T(8,128)(2,1)S(1)} %fusion.25, bf16[8,24,128]{2,0,1:T(8,128)(2,1)S(1)} %get-tuple-element.29, bf16[8,2,128]{2,0,1:T(8,128)(2,1)S(1)} %collective-permute-done.2, ...), kind=kOutput, calls=%fused_computation.25 | convolution fusion | flops 6463488 | bytes 1040504 | tf_op jit(solution)/shard_map/fbj,bij->fbi/dot_general | solution.py:53
  15.6 1.7 %convolution_add_fusion.9 = f32[24,8,128]{2,1,0:T(8,128)S(1)} fusion(f32[24,8,128]{2,1,0:T(8,128)S(1)} %fusion.11, bf16[5,24,128,128]{3,2,1,0:T(8,128)(2,1)} %param.9, bf16[8,24,128]{2,0,1:T(8,128)(2,1)S(1)} %get-tuple-element.30, bf16[8,24,128]{2,0,1:T(8,128)(2,1)S(1)} %fusion.25, bf16[8,24,128]{2,0,1:T(8,128)(2,1)S(1)} %get-tuple-element.29, ...), kind=kOutput, calls=%fused_computation.16 | convolution fusion | flops 6488064 | bytes 1138808 | tf_op jit(solution)/shard_map/fbj,bij->fbi/dot_general | solution.py:53
  17.3 1.7 %convolution_add_fusion.8 = f32[24,8,128]{2,1,0:T(8,128)S(1)} fusion(f32[24,8,128]{2,1,0:T(8,128)S(1)} %convolution_add_fusion.9, bf16[5,24,128,128]{3,2,1,0:T(8,128)(2,1)} %param.9, bf16[8,24,128]{2,0,1:T(8,128)(2,1)S(1)} %get-tuple-element.30, bf16[8,24,128]{2,0,1:T(8,128)(2,1)S(1)} %fusion.25, bf16[8,24,128]{2,0,1:T(8,128)(2,1)S(1)} %get-tuple-element.29, ...), kind=kOutput, calls=%fused_computation.15 | convolution fusion | flops 6488064 | bytes 1138808 | tf_op jit(solution)/shard_map/fbj,bij->fbi/dot_general | solution.py:53
  19.0 1.7 %convolution_add_fusion.7 = f32[24,8,128]{2,1,0:T(8,128)S(1)} fusion(f32[24,8,128]{2,1,0:T(8,128)S(1)} %convolution_add_fusion.8, bf16[5,24,128,128]{3,2,1,0:T(8,128)(2,1)} %param.9, bf16[8,24,128]{2,0,1:T(8,128)(2,1)S(1)} %get-tuple-element.30, bf16[8,24,128]{2,0,1:T(8,128)(2,1)S(1)} %fusion.25, bf16[8,24,128]{2,0,1:T(8,128)(2,1)S(1)} %get-tuple-element.29, ...), kind=kOutput, calls=%fused_computation.14 | convolution fusion | flops 6488064 | bytes 1138808 | tf_op jit(solution)/shard_map/fbj,bij->fbi/dot_general | solution.py:53
  20.8 1.7 %fusion.38 = f32[8,24,128]{2,0,1:T(8,128)S(1)} fusion(f32[7,24,128]{2,0,1:T(8,128)S(1)} %copy.33, f32[1,24,128]{2,0,1:T(1,128)S(1)} %bitcast.251, f32[8,24,128]{2,1,0:T(8,128)S(1)} %copy-done.4, f32[24,8,128]{2,1,0:T(8,128)S(1)} %convolution_add_fusion.7, bf16[5,24,128,128]{3,2,1,0:T(8,128)(2,1)} %param.9, bf16[8,24,128]{2,0,1:T(8,128)(2,1)S(1)} %get-tuple-element.30, ...), kind=kOutput, calls=%fused_computation.80 | convolution fusion | flops 6635520 | bytes 1433752 | tf_op jit(solution)/shard_map/fbj,bij->fbi/dot_general | solution.py:53
  22.5 1.8 %collective-permute-start.3 = (f32[2,8,24,128]{3,1,2,0:T(8,128)S(1)}, f32[2,8,24,128]{3,1,2,0:T(8,128)S(1)}, u32[]{:S(2)}, u32[]{:S(2)}) collective-permute-start(f32[2,8,24,128]{3,1,2,0:T(8,128)S(1)} %stack.52), channel_id=1, source_target_pairs={{0,16},{16,0},{4,20},{20,4},{8,24},{24,8},{12,28},{28,12},{1,17},{... | collective-permute-start | bytes 589832 | tf_op jit(solution)/shard_map/ppermute | solution.py:42
  24.4 5.3 %collective-permute-done.3 = f32[2,8,24,128]{3,1,2,0:T(8,128)S(1)} collective-permute-done((f32[2,8,24,128]{3,1,2,0:T(8,128)S(1)}, f32[2,8,24,128]{3,1,2,0:T(8,128)S(1)}, u32[]{:S(2)}, u32[]{:S(2)}) %collective-permute-start.3) | collective-permute-done | bytes 196640 | tf_op jit(solution)/shard_map/ppermute | solution.py:42
  29.8 1.6 %collective-permute-start.4 = (f32[2,8,24,128]{3,1,2,0:T(8,128)S(1)}, f32[2,8,24,128]{3,1,2,0:T(8,128)S(1)}, u32[]{:S(2)}, u32[]{:S(2)}) collective-permute-start(f32[2,8,24,128]{3,1,2,0:T(8,128)S(1)} %pad_maximum_fusion), channel_id=1, source_target_pairs={{0,8},{8,0},{4,12},{12,4},{16,24},{24,16},{20,28},{28,20},{1,9},{9... | collective-permute-start | bytes 589832 | tf_op jit(solution)/shard_map/ppermute | solution.py:42
  31.6 4.6 %collective-permute-done.4 = f32[2,8,24,128]{3,1,2,0:T(8,128)S(1)} collective-permute-done((f32[2,8,24,128]{3,1,2,0:T(8,128)S(1)}, f32[2,8,24,128]{3,1,2,0:T(8,128)S(1)}, u32[]{:S(2)}, u32[]{:S(2)}) %collective-permute-start.4) | collective-permute-done | bytes 196640 | tf_op jit(solution)/shard_map/ppermute | solution.py:42
  36.4 1.4 %collective-permute-done.5 = f32[2,8,24,128]{3,1,2,0:T(8,128)S(1)} collective-permute-done((f32[2,8,24,128]{3,1,2,0:T(8,128)S(1)}, f32[2,8,24,128]{3,1,2,0:T(8,128)S(1)}, u32[]{:S(2)}, u32[]{:S(2)}) %collective-permute-start.5) | collective-permute-done | bytes 196640 | tf_op jit(solution)/shard_map/ppermute | solution.py:42
  39.9 1.3 %collective-permute-start.6 = (bf16[16,2,128]{2,0,1:T(8,128)(2,1)S(1)}, bf16[16,2,128]{2,0,1:T(8,128)(2,1)S(1)}, u32[]{:S(2)}, u32[]{:S(2)}) collective-permute-start(bf16[16,2,128]{2,0,1:T(8,128)(2,1)S(1)} %get-tuple-element.27), channel_id=1, source_target_pairs={{1,0},{2,1},{3,2},{5,4},{6,5},{7,6},{9,8},{10,9},{11,10},{13,12},{... | collective-permute-start | bytes 24584 | tf_op jit(solution)/shard_map/ppermute | solution.py:30
  41.2 5.0 %collective-permute-start.7 = (bf16[16,2,128]{2,0,1:T(8,128)(2,1)S(1)}, bf16[16,2,128]{2,0,1:T(8,128)(2,1)S(1)}, u32[]{:S(2)}, u32[]{:S(2)}) collective-permute-start(bf16[16,2,128]{2,0,1:T(8,128)(2,1)S(1)} %get-tuple-element.28), channel_id=1, source_target_pairs={{0,1},{1,2},{2,3},{4,5},{5,6},{6,7},{8,9},{9,10},{10,11},{12,13},{... | collective-permute-start | bytes 24584 | tf_op jit(solution)/shard_map/ppermute | solution.py:27
  46.2 1.3 %collective-permute-done.7 = bf16[16,2,128]{2,0,1:T(8,128)(2,1)S(1)} collective-permute-done((bf16[16,2,128]{2,0,1:T(8,128)(2,1)S(1)}, bf16[16,2,128]{2,0,1:T(8,128)(2,1)S(1)}, u32[]{:S(2)}, u32[]{:S(2)}) %collective-permute-start.7) | collective-permute-done | bytes 8224 | tf_op jit(solution)/shard_map/ppermute | solution.py:27
  48.2 0.6 convolution_add_fusion.3
  48.7 0.6 convolution_add_fusion.2
  49.3 0.6 convolution_add_fusion.1
  49.9 0.6 fusion
  52.5 1.4 %collective-permute-done.8 = f32[2,8,24,128]{3,1,2,0:T(8,128)S(1)} collective-permute-done((f32[2,8,24,128]{3,1,2,0:T(8,128)S(1)}, f32[2,8,24,128]{3,1,2,0:T(8,128)S(1)}, u32[]{:S(2)}, u32[]{:S(2)}) %collective-permute-start.8) | collective-permute-done | bytes 196640 | tf_op jit(solution)/shard_map/ppermute | solution.py:42
  54.0 1.4 %collective-permute-start.9 = (f32[2,8,24,128]{3,1,2,0:T(8,128)S(1)}, f32[2,8,24,128]{3,1,2,0:T(8,128)S(1)}, u32[]{:S(2)}, u32[]{:S(2)}) collective-permute-start(f32[2,8,24,128]{3,1,2,0:T(8,128)S(1)} %pad_maximum_fusion.3), channel_id=1, source_target_pairs={{0,8},{8,0},{4,12},{12,4},{16,24},{24,16},{20,28},{28,20},{1,9},{9... | collective-permute-start | bytes 589832 | tf_op jit(solution)/shard_map/ppermute | solution.py:42
  55.4 5.6 %collective-permute-done.9 = f32[2,8,24,128]{3,1,2,0:T(8,128)S(1)} collective-permute-done((f32[2,8,24,128]{3,1,2,0:T(8,128)S(1)}, f32[2,8,24,128]{3,1,2,0:T(8,128)S(1)}, u32[]{:S(2)}, u32[]{:S(2)}) %collective-permute-start.9) | collective-permute-done | bytes 196640 | tf_op jit(solution)/shard_map/ppermute | solution.py:42
  61.1 1.4 %collective-permute-start.10 = (f32[2,8,24,128]{3,1,2,0:T(8,128)S(1)}, f32[2,8,24,128]{3,1,2,0:T(8,128)S(1)}, u32[]{:S(2)}, u32[]{:S(2)}) collective-permute-start(f32[2,8,24,128]{3,1,2,0:T(8,128)S(1)} %pad_maximum_fusion.4), channel_id=1, source_target_pairs={{0,16},{16,0},{4,20},{20,4},{8,24},{24,8},{12,28},{28,12},{1,17},{... | collective-permute-start | bytes 589832 | tf_op jit(solution)/shard_map/ppermute | solution.py:42
  62.5 4.8 %collective-permute-done.10 = f32[2,8,24,128]{3,1,2,0:T(8,128)S(1)} collective-permute-done((f32[2,8,24,128]{3,1,2,0:T(8,128)S(1)}, f32[2,8,24,128]{3,1,2,0:T(8,128)S(1)}, u32[]{:S(2)}, u32[]{:S(2)}) %collective-permute-start.10) | collective-permute-done | bytes 196640 | tf_op jit(solution)/shard_map/ppermute | solution.py:42
  67.4 0.7 copy.18
  (54 shorter events, 5.3 us)
Async XLA Ops:
  0.0 39.2 %copy-start = (bf16[24,128,128]{2,1,0:T(8,128)(2,1)S(1)}, bf16[24,128,128]{2,1,0:T(8,128)(2,1)}, u32[]{:S(2)}) copy-start(bf16[24,128,128]{2,1,0:T(8,128)(2,1)} %param.10) | copy-start | bytes 2359300
  0.0 20.8 %copy-start.1 = (f32[8,24,128]{2,1,0:T(8,128)S(1)}, f32[8,24,128]{2,1,0:T(8,128)}, u32[]{:S(2)}) copy-start(f32[8,24,128]{2,1,0:T(8,128)} %param.6) | copy-start | bytes 294916
  0.0 20.7 %copy-start.2 = (f32[24,128]{1,0:T(8,128)S(1)}, f32[24,128]{1,0:T(8,128)}, u32[]{:S(2)}) copy-start(f32[24,128]{1,0:T(8,128)} %param.8) | copy-start | bytes 36868
  0.0 20.8 %copy-start.4 = (f32[8,24,128]{2,1,0:T(8,128)S(1)}, f32[8,24,128]{2,1,0:T(8,128)}, u32[]{:S(2)}) copy-start(f32[8,24,128]{2,1,0:T(8,128)} %param.7) | copy-start | bytes 294916
  0.8 19.9 %collective-permute-start = (f32[1,24,128]{2,0,1:T(1,128)S(1)}, f32[1,24,128]{2,0,1:T(1,128)S(1)}, u32[]{:S(2)}, u32[]{:S(2)}) collective-permute-start(f32[1,24,128]{2,0,1:T(1,128)S(1)} %bitcast.248), channel_id=1, source_target_pairs={{0,4},{4,8},{8,12},{12,16},{16,20},{20,24},{24,28},{1,5},{5,9},{9,... | collective-permute-start | bytes 36872 | tf_op jit(solution)/shard_map/ppermute | solution.py:19
  4.1 8.3 %collective-permute-start.2 = (bf16[8,2,128]{2,0,1:T(8,128)(2,1)S(1)}, bf16[8,2,128]{2,0,1:T(8,128)(2,1)S(1)}, u32[]{:S(2)}, u32[]{:S(2)}) collective-permute-start(bf16[8,2,128]{2,0,1:T(8,128)(2,1)S(1)} %get-tuple-element.31), channel_id=1, source_target_pairs={{0,1},{1,2},{2,3},{4,5},{5,6},{6,7},{8,9},{9,10},{10,11},{12,13},{... | collective-permute-start | bytes 12296 | tf_op jit(solution)/shard_map/ppermute | solution.py:27
  8.4 5.5 %collective-permute-start.1 = (bf16[8,2,128]{2,0,1:T(8,128)(2,1)S(1)}, bf16[8,2,128]{2,0,1:T(8,128)(2,1)S(1)}, u32[]{:S(2)}, u32[]{:S(2)}) collective-permute-start(bf16[8,2,128]{2,0,1:T(8,128)(2,1)S(1)} %get-tuple-element.32), channel_id=1, source_target_pairs={{1,0},{2,1},{3,2},{5,4},{6,5},{7,6},{9,8},{10,9},{11,10},{13,12},{... | collective-permute-start | bytes 12296 | tf_op jit(solution)/shard_map/ppermute | solution.py:30
  22.5 7.2 %collective-permute-start.3 = (f32[2,8,24,128]{3,1,2,0:T(8,128)S(1)}, f32[2,8,24,128]{3,1,2,0:T(8,128)S(1)}, u32[]{:S(2)}, u32[]{:S(2)}) collective-permute-start(f32[2,8,24,128]{3,1,2,0:T(8,128)S(1)} %stack.52), channel_id=1, source_target_pairs={{0,16},{16,0},{4,20},{20,4},{8,24},{24,8},{12,28},{28,12},{1,17},{... | collective-permute-start | bytes 589832 | tf_op jit(solution)/shard_map/ppermute | solution.py:42
  29.8 6.4 %collective-permute-start.4 = (f32[2,8,24,128]{3,1,2,0:T(8,128)S(1)}, f32[2,8,24,128]{3,1,2,0:T(8,128)S(1)}, u32[]{:S(2)}, u32[]{:S(2)}) collective-permute-start(f32[2,8,24,128]{3,1,2,0:T(8,128)S(1)} %pad_maximum_fusion), channel_id=1, source_target_pairs={{0,8},{8,0},{4,12},{12,4},{16,24},{24,16},{20,28},{28,20},{1,9},{9... | collective-permute-start | bytes 589832 | tf_op jit(solution)/shard_map/ppermute | solution.py:42
  31.5 16.1 %copy-start.3 = (bf16[5,24,128,128]{3,2,1,0:T(8,128)(2,1)S(1)}, bf16[5,24,128,128]{3,2,1,0:T(8,128)(2,1)}, u32[]{:S(2)}) copy-start(bf16[5,24,128,128]{3,2,1,0:T(8,128)(2,1)} %param.9) | copy-start | bytes 11796484
  36.3 1.5 %collective-permute-start.5 = (f32[2,8,24,128]{3,1,2,0:T(8,128)S(1)}, f32[2,8,24,128]{3,1,2,0:T(8,128)S(1)}, u32[]{:S(2)}, u32[]{:S(2)}) collective-permute-start(f32[2,8,24,128]{3,1,2,0:T(8,128)S(1)} %pad_maximum_fusion.1), channel_id=1, source_target_pairs={{0,4},{4,0},{8,12},{12,8},{16,20},{20,16},{24,28},{28,24},{1,5},{5... | collective-permute-start | bytes 589832 | tf_op jit(solution)/shard_map/ppermute | solution.py:42
  39.9 6.3 %collective-permute-start.6 = (bf16[16,2,128]{2,0,1:T(8,128)(2,1)S(1)}, bf16[16,2,128]{2,0,1:T(8,128)(2,1)S(1)}, u32[]{:S(2)}, u32[]{:S(2)}) collective-permute-start(bf16[16,2,128]{2,0,1:T(8,128)(2,1)S(1)} %get-tuple-element.27), channel_id=1, source_target_pairs={{1,0},{2,1},{3,2},{5,4},{6,5},{7,6},{9,8},{10,9},{11,10},{13,12},{... | collective-permute-start | bytes 24584 | tf_op jit(solution)/shard_map/ppermute | solution.py:30
  41.2 6.4 %collective-permute-start.7 = (bf16[16,2,128]{2,0,1:T(8,128)(2,1)S(1)}, bf16[16,2,128]{2,0,1:T(8,128)(2,1)S(1)}, u32[]{:S(2)}, u32[]{:S(2)}) collective-permute-start(bf16[16,2,128]{2,0,1:T(8,128)(2,1)S(1)} %get-tuple-element.28), channel_id=1, source_target_pairs={{0,1},{1,2},{2,3},{4,5},{5,6},{6,7},{8,9},{9,10},{10,11},{12,13},{... | collective-permute-start | bytes 24584 | tf_op jit(solution)/shard_map/ppermute | solution.py:27
  52.4 1.5 %collective-permute-start.8 = (f32[2,8,24,128]{3,1,2,0:T(8,128)S(1)}, f32[2,8,24,128]{3,1,2,0:T(8,128)S(1)}, u32[]{:S(2)}, u32[]{:S(2)}) collective-permute-start(f32[2,8,24,128]{3,1,2,0:T(8,128)S(1)} %pad_maximum_fusion.2), channel_id=1, source_target_pairs={{0,4},{4,0},{8,12},{12,8},{16,20},{20,16},{24,28},{28,24},{1,5},{5... | collective-permute-start | bytes 589832 | tf_op jit(solution)/shard_map/ppermute | solution.py:42
  54.0 7.0 %collective-permute-start.9 = (f32[2,8,24,128]{3,1,2,0:T(8,128)S(1)}, f32[2,8,24,128]{3,1,2,0:T(8,128)S(1)}, u32[]{:S(2)}, u32[]{:S(2)}) collective-permute-start(f32[2,8,24,128]{3,1,2,0:T(8,128)S(1)} %pad_maximum_fusion.3), channel_id=1, source_target_pairs={{0,8},{8,0},{4,12},{12,4},{16,24},{24,16},{20,28},{28,20},{1,9},{9... | collective-permute-start | bytes 589832 | tf_op jit(solution)/shard_map/ppermute | solution.py:42
  61.1 6.2 %collective-permute-start.10 = (f32[2,8,24,128]{3,1,2,0:T(8,128)S(1)}, f32[2,8,24,128]{3,1,2,0:T(8,128)S(1)}, u32[]{:S(2)}, u32[]{:S(2)}) collective-permute-start(f32[2,8,24,128]{3,1,2,0:T(8,128)S(1)} %pad_maximum_fusion.4), channel_id=1, source_target_pairs={{0,16},{16,0},{4,20},{20,4},{8,24},{24,8},{12,28},{28,12},{1,17},{... | collective-permute-start | bytes 589832 | tf_op jit(solution)/shard_map/ppermute | solution.py:42
where the time goes:
time: 68.6 us; the launch traced here: 68.1 us
  waiting for transfers between devices  25.9 us (38%)
  starting transfers between devices  20.5 us (30%)
  matrix products  14.8 us (22%)
  other arithmetic  3.69 us (5%)
  local copies, waits for them, and re-layouts  2.42 us (4%)
  between operations  0.69 us (1%)
    ppermute x6, waiting for transfers between devices, from_partner(): return lax.ppermute(block, axis, route)  23.1 us
    dot_general x10, matrix products, apply_padded(): jnp.einsum('fbj,bij->fbi', chosen, blocks[column], preferred_element_type...  11.3 us
    ppermute x2, starting transfers between devices, extended(): lax.ppermute(lax.slice_in_dim(block, block.shape[dim] - width, None, axis...  9.3 us
    ppermute x6, starting transfers between devices, from_partner(): return lax.ppermute(block, axis, route)  6.24 us
    ppermute x2, starting transfers between devices, extended(): lax.ppermute(lax.slice_in_dim(block, 0, width, axis=dim), axis, backward)  2.58 us
    ppermute x1, starting transfers between devices, from_behind(): return lax.ppermute(block, axis, route)  2.35 us
    eq x2, other arithmetic, apply_padded(): picked = (couple[:, column] == offset)[None, :, None]  1.77 us
    ppermute x2, waiting for transfers between devices, extended(): lax.ppermute(lax.slice_in_dim(block, 0, width, axis=dim), axis, backward)  1.48 us
  transfers between devices with their start and end apart: 11, of which 8 were waited for; matrix products, arithmetic and copies ran while one was open for 15% of the time, Pallas kernels for 0%

commit v1 on v0

--- a/solution.py
+++ b/solution.py
@@ -1,8 +1,12 @@
+import functools
 import math
 
 import jax
 import jax.numpy as jnp
+import numpy as np
 from jax import lax
+from jax.experimental import pallas as pl
+from jax.experimental.pallas import tpu as pltpu
 from jax.sharding import PartitionSpec as P
 
 SWEEPS = 2
@@ -57,7 +61,7 @@
     return total
 
 
-def on_device(state, forcing, initial, blocks, precond, couple):
+def on_device_steps(state, forcing, initial, blocks, precond, couple):
     local_steps = state.shape[0]
     devices_tm = lax.axis_size("tm")
     position = lax.axis_index("tm")
@@ -165,6 +169,459 @@
     return state + change
 
 
+MESH = pl.DeviceIdType.MESH
+NT_DIMS = (((1,), (1,)), ((), ()))
+HIGHEST = lax.Precision.HIGHEST
+
+
+def tables(steps):
+    half = steps // 2
+    rate = math.exp(math.log(alpha_rate) / steps)
+    step = np.arange(steps)
+    freq = np.arange(half)
+    angle = 2.0 * np.pi * ((freq[:, None] * step[None, :]) % steps) / steps
+    cosine, sine = np.cos(angle), np.sin(angle)
+    nyquist = 1.0 - 2.0 * (step % 2)
+    forward = np.concatenate([cosine, nyquist[None], -sine[1:]], 0) * rate**step
+    inverse = np.concatenate([2.0 * cosine, nyquist[None], -2.0 * sine[1:]], 0)
+    inverse[0] = 1.0
+    inverse = inverse.T / steps * (rate ** (-step))[:, None]
+    theta = 2.0 * np.pi * np.arange(half + 1) / steps
+    lam = 1.0 - rate * np.exp(-1j * theta)
+    lam[half] = lam[half].real
+    coef = relaxation / (1.0 + lam)
+
+    def columns(factor):
+        real = np.concatenate([factor.real[:half], factor.real[half:], factor.real[1:half]])
+        imag = np.concatenate([[0.0], factor.imag[1:half]])
+        return real, np.concatenate([-imag, imag])
+
+    coef_own, coef_swap = columns(coef)
+    lam_own, lam_swap = columns(lam * coef)
+    swap = np.roll(np.eye(steps), half, 1)
+    inverse = inverse @ (np.diag(coef_own) + np.diag(coef_swap) @ swap)
+    factors = np.zeros((steps, steps))
+    lanes = -(-steps // 128) * 128
+    for place, column in enumerate((coef_own, coef_swap, lam_own, lam_swap)):
+        factors[:, place] = column
+    stacked = np.stack([forward, inverse, factors])
+    return np.pad(stacked, ((0, 0), (0, 0), (0, lanes - steps))).astype(np.float32)
+
+
+def kernel(
+    sizes,
+    state_h,
+    forcing_h,
+    initial_h,
+    blocks_h,
+    precond_h,
+    couple_s,
+    table_h,
+    out_ref,
+    state_v,
+    forcing_v,
+    initial_v,
+    wb,
+    wp,
+    table_v,
+    chunk,
+    edge,
+    diff,
+    rq,
+    rd,
+    redge,
+    xsq,
+    xsol,
+    back,
+    rback,
+    local_sem,
+    q_send,
+    q_recv,
+    d_send,
+    d_recv,
+    edge_send,
+    edge_recv,
+    halo_send,
+    halo_recv,
+    b_send,
+    b_recv,
+):
+    nt, ns, steps, width, own = sizes
+    total = nt * steps
+    half = total // 2
+    t = lax.axis_index("tm")
+    s = lax.axis_index("space")
+    first, last = t == 0, t == nt - 1
+    below, above = s > 0, s < ns - 1
+    lower, upper = jnp.maximum(s - 1, 0), jnp.minimum(s + 1, ns - 1)
+    low_edge = jnp.logical_and(first, below)
+    high_edge = jnp.logical_and(last, above)
+
+    barrier = pltpu.get_barrier_semaphore()
+    for o in range(1, nt):
+        pl.semaphore_signal(
+            barrier, inc=1, device_id=(lax.rem(t + o, nt), s), device_id_type=MESH
+        )
+
+    @pl.when(low_edge)
+    def _():
+        for o in range(nt):
+            pl.semaphore_signal(barrier, inc=1, device_id=(o, lower), device_id_type=MESH)
+
+    @pl.when(high_edge)
+    def _():
+        for o in range(nt):
+            pl.semaphore_signal(barrier, inc=1, device_id=(o, upper), device_id_type=MESH)
+
+    start = t * own
+    loads = [
+        pltpu.make_async_copy(source, target, local_sem.at[place])
+        for place, (source, target) in enumerate(
+            (
+                (state_h, state_v),
+                (forcing_h, forcing_v),
+                (initial_h, initial_v),
+                (blocks_h.at[:, pl.ds(start, own)], wb),
+                (table_h, table_v),
+                (precond_h.at[pl.ds(start, own)], wp),
+            )
+        )
+    ]
+    for load in loads:
+        load.start()
+
+    loads[0].wait()
+    state = state_v[...]
+    by_block = jnp.swapaxes(state, 0, 1)
+    squares = 0.5 * by_block * by_block
+    blank = jnp.zeros((steps, squares.shape[2]), jnp.float32)
+    for target in range(nt):
+        parts = []
+        for j in range(own * target - 2, own * (target + 1) + 2):
+            parts.append(squares[j] if 0 <= j < width else blank)
+        tail = state[steps - 1, own * target : own * (target + 1)]
+        tail_hi = tail.astype(jnp.bfloat16).astype(jnp.float32)
+        parts += [tail_hi, tail - tail_hi]
+        if steps > 2 * own:
+            parts.append(blank[: steps - 2 * own])
+        chunk[target] = jnp.concatenate(parts, 0).astype(jnp.bfloat16)
+    edge[0] = jnp.concatenate([squares[width - 2], squares[width - 1]], 0).astype(jnp.bfloat16)
+    edge[1] = jnp.concatenate([squares[0], squares[1]], 0).astype(jnp.bfloat16)
+
+    signals = nt - 1 + jnp.where(below, 1, 0) + jnp.where(above, 1, 0)
+    pl.semaphore_wait(barrier, signals)
+
+    q_copies = []
+    for o in range(1, nt):
+        target = lax.rem(t + o, nt)
+        q_copies.append(
+            pltpu.make_async_remote_copy(
+                src_ref=chunk.at[target],
+                dst_ref=rq.at[t],
+                send_sem=q_send.at[o],
+                recv_sem=q_recv.at[o],
+                device_id=(target, s),
+                device_id_type=MESH,
+            )
+        )
+    for copy in q_copies:
+        copy.start()
+    edge_up = pltpu.make_async_remote_copy(
+        src_ref=edge.at[0],
+        dst_ref=redge.at[t],
+        send_sem=edge_send.at[0],
+        recv_sem=edge_recv.at[t],
+        device_id=(0, upper),
+        device_id_type=MESH,
+    )
+    edge_down = pltpu.make_async_remote_copy(
+        src_ref=edge.at[1],
+        dst_ref=redge.at[t],
+        send_sem=edge_send.at[1],
+        recv_sem=edge_recv.at[t],
+        device_id=(nt - 1, lower),
+        device_id_type=MESH,
+    )
+
+    @pl.when(above)
+    def _():
+        edge_up.start()
+
+    @pl.when(below)
+    def _():
+        edge_down.start()
+
+    loads[1].wait()
+    loads[2].wait()
+    forcing = forcing_v[...]
+    initial = jnp.where(first, initial_v[...], 0.0)
+    previous = jnp.concatenate([initial[None], state[:-1]], 0)
+    diff[...] = jnp.swapaxes(forcing - state + previous, 0, 1)
+    d_copies = []
+    for o in range(1, nt):
+        target = lax.rem(t + o, nt)
+        d_copies.append(
+            pltpu.make_async_remote_copy(
+                src_ref=diff.at[pl.ds(target * own, own)],
+                dst_ref=rd.at[t],
+                send_sem=d_send.at[o],
+                recv_sem=d_recv.at[o],
+                device_id=(target, s),
+                device_id_type=MESH,
+            )
+        )
+    for copy in d_copies:
+        copy.start()
+    rq[t] = chunk[t]
+    rd[t] = diff[pl.ds(start, own)]
+
+    for copy in q_copies:
+        copy.wait_recv()
+    got = [rq[source].astype(jnp.float32) for source in range(nt)]
+    for e in range(own + 4):
+        xsq[e] = jnp.concatenate(
+            [part[e * steps : (e + 1) * steps] for part in got], 0
+        ).astype(jnp.bfloat16)
+    lead = (own + 4) * steps
+    tails = [
+        part[lead : lead + own] + part[lead + own : lead + 2 * own] for part in got[:-1]
+    ]
+
+    def take_edge(place):
+        for source in range(nt):
+            pltpu.make_async_remote_copy(
+                src_ref=edge.at[0],
+                dst_ref=redge.at[source],
+                send_sem=edge_send.at[0],
+                recv_sem=edge_recv.at[source],
+                device_id=(0, 0),
+                device_id_type=MESH,
+            ).wait_recv()
+        edges = [redge[source].astype(jnp.float32) for source in range(nt)]
+        for e in range(2):
+            xsq[place + e] = jnp.concatenate(
+                [part[e * steps : (e + 1) * steps] for part in edges], 0
+            ).astype(jnp.bfloat16)
+
+    @pl.when(low_edge)
+    def _():
+        take_edge(0)
+
+    @pl.when(high_edge)
+    def _():
+        take_edge(own + 2)
+
+    loads[3].wait()
+
+    def coupled(field, e):
+        slots = wb.shape[0]
+        rows = [field[e + 2 + couple_s[start + e, slot]] for slot in range(slots)]
+        weights = [wb[slot, e] for slot in range(slots)]
+        return lax.dot_general(
+            jnp.concatenate(rows, 1),
+            jnp.concatenate(weights, 1),
+            NT_DIMS,
+            preferred_element_type=jnp.float32,
+        )
+
+    def conditioned(rounded):
+        size = wp.shape[1]
+        return jnp.concatenate(
+            [
+                lax.dot_general(
+                    rounded[:, e * size : (e + 1) * size],
+                    wp[e],
+                    NT_DIMS,
+                    preferred_element_type=jnp.float32,
+                )
+                for e in range(own)
+            ],
+            1,
+        )
+
+    flux = [coupled(xsq, e) for e in range(own)]
+    for copy in d_copies:
+        copy.wait_recv()
+    leading = lax.broadcasted_iota(jnp.int32, blank.shape, 0) == 0
+    residual = []
+    for e in range(own):
+        parts = [rd[0, e]]
+        for source in range(1, nt):
+            carried = jnp.broadcast_to(tails[source - 1][e : e + 1], blank.shape)
+            parts.append(rd[source, e] + jnp.where(leading, carried, 0.0))
+        residual.append(jnp.concatenate(parts, 0) - time_step * flux[e])
+    loads[4].wait()
+    spectrum = jnp.dot(
+        table_v[0][:, :total],
+        jnp.concatenate(residual, 1),
+        precision=HIGHEST,
+        preferred_element_type=jnp.float32,
+    )
+
+    loads[5].wait()
+    first_step = conditioned(spectrum.astype(jnp.bfloat16))
+    swapped = jnp.concatenate([first_step[half:], first_step[:half]], 0)
+    factors = table_v[2]
+    sol = factors[:, 0:1] * first_step + factors[:, 1:2] * swapped
+    size = wp.shape[1]
+    for e in range(own):
+        xsol[2 + e] = sol[:, e * size : (e + 1) * size].astype(jnp.bfloat16)
+
+    has_down = jnp.logical_or(t > 0, below)
+    has_up = jnp.logical_or(t < nt - 1, above)
+    halo_down = pltpu.make_async_remote_copy(
+        src_ref=xsol.at[pl.ds(2, 2)],
+        dst_ref=xsol.at[pl.ds(own + 2, 2)],
+        send_sem=halo_send.at[0],
+        recv_sem=halo_recv.at[0],
+        device_id=(jnp.where(first, nt - 1, t - 1), jnp.where(first, lower, s)),
+        device_id_type=MESH,
+    )
+    halo_up = pltpu.make_async_remote_copy(
+        src_ref=xsol.at[pl.ds(own, 2)],
+        dst_ref=xsol.at[pl.ds(0, 2)],
+        send_sem=halo_send.at[1],
+        recv_sem=halo_recv.at[1],
+        device_id=(jnp.where(last, 0, t + 1), jnp.where(last, upper, s)),
+        device_id_type=MESH,
+    )
+
+    @pl.when(has_down)
+    def _():
+        halo_down.start()
+
+    @pl.when(has_up)
+    def _():
+        halo_up.start()
+
+    @pl.when(jnp.logical_not(has_down))
+    def _():
+        xsol[0:2] = jnp.zeros((2,) + xsol.shape[1:], jnp.bfloat16)
+
+    @pl.when(jnp.logical_not(has_up))
+    def _():
+        xsol[own + 2 : own + 4] = jnp.zeros((2,) + xsol.shape[1:], jnp.bfloat16)
+
+    left = spectrum - (factors[:, 2:3] * first_step + factors[:, 3:4] * swapped)
+
+    @pl.when(has_down)
+    def _():
+        halo_up.wait_recv()
+
+    @pl.when(has_up)
+    def _():
+        halo_down.wait_recv()
+
+    applied = jnp.concatenate([coupled(xsol, e) for e in range(own)], 1)
+    left = left - time_step * applied
+    steps_sum = first_step + conditioned(left.astype(jnp.bfloat16))
+    change = jnp.dot(
+        table_v[1][:, :total], steps_sum, precision=HIGHEST, preferred_element_type=jnp.float32
+    )
+    for e in range(own):
+        back[e] = change[:, e * size : (e + 1) * size]
+    b_copies = []
+    for o in range(1, nt):
+        target = lax.rem(t + o, nt)
+        b_copies.append(
+            pltpu.make_async_remote_copy(
+                src_ref=back.at[:, pl.ds(pl.multiple_of(target * steps, steps), steps)],
+                dst_ref=rback.at[pl.ds(start, own)],
+                send_sem=b_send.at[o],
+                recv_sem=b_recv.at[o],
+                device_id=(target, s),
+                device_id_type=MESH,
+            )
+        )
+    for copy in b_copies:
+        copy.start()
+    rback[pl.ds(start, own)] = back[:, pl.ds(pl.multiple_of(t * steps, steps), steps)]
+    for copy in b_copies:
+        copy.wait_recv()
+    out_ref[...] = jnp.swapaxes(rback[...], 0, 1)
+
+    for copy in q_copies + d_copies + b_copies:
+        copy.wait_send()
+
+    @pl.when(above)
+    def _():
+        edge_up.wait_send()
+
+    @pl.when(below)
+    def _():
+        edge_down.wait_send()
+
+    @pl.when(has_down)
+    def _():
+        halo_down.wait_send()
+
+    @pl.when(has_up)
+    def _():
+        halo_up.wait_send()
+
+
+def on_device_blocks(state, forcing, initial, blocks, precond, couple):
+    nt, ns = lax.axis_size("tm"), lax.axis_size("space")
+    steps, width, size = state.shape
+    own = width // nt
+    total = nt * steps
+    slots = blocks.shape[0]
+    table = jnp.asarray(tables(total))
+    anywhere = pl.BlockSpec(memory_space=pl.ANY)
+    rows = (own + 5) * steps
+    f32, b16 = jnp.float32, jnp.bfloat16
+    dma = pltpu.SemaphoreType.DMA
+    change = pl.pallas_call(
+        functools.partial(kernel, (nt, ns, steps, width, own)),
+        out_shape=jax.ShapeDtypeStruct(state.shape, f32),
+        in_specs=[anywhere] * 5 + [pl.BlockSpec(memory_space=pltpu.SMEM), anywhere],
+        out_specs=pl.BlockSpec(memory_space=pltpu.VMEM),
+        scratch_shapes=[
+            pltpu.VMEM(state.shape, f32),
+            pltpu.VMEM(state.shape, f32),
+            pltpu.VMEM(initial.shape, f32),
+            pltpu.VMEM((slots, own, size, size), b16),
+            pltpu.VMEM((own, size, size), b16),
+            pltpu.VMEM(table.shape, f32),
+            pltpu.VMEM((nt, rows, size), b16),
+            pltpu.VMEM((2, 2 * steps, size), b16),
+            pltpu.VMEM((width, steps, size), f32),
+            pltpu.VMEM((nt, rows, size), b16),
+            pltpu.VMEM((nt, own, steps, size), f32),
+            pltpu.VMEM((nt, 2 * steps, size), b16),
+            pltpu.VMEM((own + 4, total, size), b16),
+            pltpu.VMEM((own + 4, total, size), b16),
+            pltpu.VMEM((own, total, size), f32),
+            pltpu.VMEM((width, steps, size), f32),
+            dma((6,)),
+            dma((nt,)),
+            dma((nt,)),
+            dma((nt,)),
+            dma((nt,)),
+            dma((2,)),
+            dma((nt,)),
+            dma((2,)),
+            dma((2,)),
+            dma((nt,)),
+            dma((nt,)),
+        ],
+        compiler_params=pltpu.CompilerParams(
+            collective_id=0, has_side_effects=True, vmem_limit_bytes=24 * 1024 * 1024
+        ),
+    )(state, forcing, initial, blocks, precond, couple, table)
+    return state + change
+
+
+def on_device(state, forcing, initial, blocks, precond, couple):
+    nt = lax.axis_size("tm")
+    steps, width, _ = state.shape
+    own = width // nt
+    even_cut = width % nt == 0 and own >= 2 and 2 * own <= steps and steps % 8 == 0
+    if nt > 1 and even_cut and (own + 5) * steps % 16 == 0:
+        return on_device_blocks(state, forcing, initial, blocks, precond, couple)
+    return on_device_steps(state, forcing, initial, blocks, precond, couple)
+
+
 def solution(mesh):
     placed = (
         P("tm", "space", None),

time: 68.6 us -> 26.2 us (0.38)
  waiting for transfers between devices: 25.9 us -> 0 us
  starting transfers between devices: 20.5 us -> 0 us
  Pallas kernels: 0 us -> 17.7 us
  matrix products: 14.8 us -> 0 us
  local copies, waits for them, and re-layouts: 2.42 us -> 7.39 us
  other arithmetic: 3.69 us -> 0.66 us
    ppermute x11 -> x0, waiting for transfers between devices: 25.9 us -> none  [the longest x6 23.1 us: from_partner(): return lax.ppermute(block, axis, route)]
    ppermute x11 -> x0, starting transfers between devices: 20.5 us -> none  [the longest x2 9.3 us: extended(): lax.ppermute(lax.slice_in_dim(block, block.shape[dim] - width, None, axis...]
    pallas_call x0 -> x1, Pallas kernels: none -> 17.7 us  [on_device_blocks(): pl.pallas_call(functools.partial(kernel, (nt, ns, steps, width, own)), ou...]
    dot_general x20 -> x0, matrix products: 14.8 us -> none  [the longest x10 11.3 us: apply_padded(): jnp.einsum('fbj,bij->fbi', chosen, blocks[column], preferred_element_type...]
    unnamed x11 -> x13, local copies, waits for them, and re-layouts: 0.04 us -> 7.39 us
    eq x2 -> x0, other arithmetic: 1.77 us -> none  [apply_padded(): picked = (couple[:, column] == offset)[None, :, None]]
    slice x3 -> x0, local copies, waits for them, and re-layouts: 1.7 us -> none  [the longest x1 0.9 us: on_device(): previous = jnp.concatenate([first_prev, state[:-1]], 0)]
    convert_element_type x1 -> x0, other arithmetic: 0.92 us -> none  [on_device(): squares = (0.5 * state * state).astype(jnp.bfloat16)]
  transfers between devices with their start and end apart: 11 -> 0, of which waited for: 8 -> 0; matrix products, arithmetic and copies ran while one was open for 15% -> 0% of each run, Pallas kernels for 0% -> 0%
where the time goes in v1:
time: 26.2 us; the launch traced here: 25.8 us
  Pallas kernels  17.7 us (68%)
  local copies, waits for them, and re-layouts  7.39 us (28%)
  other arithmetic  0.66 us (3%)
    pallas_call x1, Pallas kernels, on_device_blocks(): pl.pallas_call(functools.partial(kernel, (nt, ns, steps, width, own)), ou...  17.7 us
    unnamed x13, local copies, waits for them, and re-layouts  7.39 us
    add x1, other arithmetic, on_device_blocks(): return state + change  0.66 us

profile of v1, /device:TPU:0, one launch (start us, length us, event | category | flops | bytes accessed | tf_op | source)
XLA Modules:
  0.0 25.8 jit_solution(17177745886637355751)
XLA Ops:
  0.0 0.8 %copy.8.couple_s = s32[24,5]{1,0:T(8,128)S(1)} copy(s32[24,5]{0,1:T(8,128)} %param.12) | data formatting | bytes 960 | tf_op args[5]
  0.8 0.0 copy-start
  0.8 2.1 %copy-done = bf16[5,24,128,128]{3,2,1,0:T(8,128)(2,1)S(1)} copy-done((bf16[5,24,128,128]{3,2,1,0:T(8,128)(2,1)S(1)}, bf16[5,24,128,128]{3,2,1,0:T(8,128)(2,1)}, u32[]{:S(2)}) %copy-start) | copy-done | bytes 3932184
  2.9 0.0 copy-start.1
  2.9 1.1 %copy-done.1 = bf16[24,128,128]{2,1,0:T(8,128)(2,1)S(1)} copy-done((bf16[24,128,128]{2,1,0:T(8,128)(2,1)S(1)}, bf16[24,128,128]{2,1,0:T(8,128)(2,1)}, u32[]{:S(2)}) %copy-start.1) | copy-done | bytes 786456
  4.0 0.0 copy-start.2
  4.0 0.9 %copy-done.2 = f32[8,24,128]{2,1,0:T(8,128)S(1)} copy-done((f32[8,24,128]{2,1,0:T(8,128)S(1)}, f32[8,24,128]{2,1,0:T(8,128)}, u32[]{:S(2)}) %copy-start.2) | copy-done | bytes 98328
  4.9 0.0 copy-start.3
  4.9 0.9 %copy-done.3 = f32[8,24,128]{2,1,0:T(8,128)S(1)} copy-done((f32[8,24,128]{2,1,0:T(8,128)S(1)}, f32[8,24,128]{2,1,0:T(8,128)}, u32[]{:S(2)}) %copy-start.3) | copy-done | bytes 98328
  5.8 0.0 copy-start.4
  5.8 0.9 %copy-done.4 = f32[3,64,128]{2,1,0:T(8,128)S(1)} copy-done((f32[3,64,128]{2,1,0:T(8,128)S(1)}, f32[3,64,128]{2,1,0:T(8,128)}, u32[]{:S(2)}) %copy-start.4) | copy-done | bytes 98328
  6.7 0.0 copy-start.5
  6.7 0.7 %copy-done.5 = f32[24,128]{1,0:T(8,128)S(1)} copy-done((f32[24,128]{1,0:T(8,128)S(1)}, f32[24,128]{1,0:T(8,128)}, u32[]{:S(2)}) %copy-start.5) | copy-done | bytes 12312
  7.4 17.7 %shard_map.73 = f32[8,24,128]{2,1,0:T(8,128)S(1)} custom-call(f32[8,24,128]{2,1,0:T(8,128)S(1)} %copy-done.2, f32[8,24,128]{2,1,0:T(8,128)S(1)} %copy-done.3, f32[24,128]{1,0:T(8,128)S(1)} %copy-done.5, bf16[5,24,128,128]{3,2,1,0:T(8,128)(2,1)S(1)} %copy-done, bf16[24,128,128]{2,1,0:T(8,128)(2,1)S(1)} %copy-done.1, s32[24,5]{1,0:T(8,128)S(1)} %copy.8.couple_s, ...), custom_call_target="tpu_custom_call" | custom-call | tf_op jit(solution)/shard_map/pallas_call | solution.py:574
  25.1 0.7 %add.3 = f32[8,24,128]{2,1,0:T(8,128)} add(f32[8,24,128]{2,1,0:T(8,128)S(1)} %copy-done.2, f32[8,24,128]{2,1,0:T(8,128)S(1)} %shard_map.73) | non-fusion elementwise | flops 24576 | bytes 294912 | tf_op jit(solution)/shard_map/add | solution.py:612
Async XLA Ops:
  0.8 2.1 %copy-start = (bf16[5,24,128,128]{3,2,1,0:T(8,128)(2,1)S(1)}, bf16[5,24,128,128]{3,2,1,0:T(8,128)(2,1)}, u32[]{:S(2)}) copy-start(bf16[5,24,128,128]{3,2,1,0:T(8,128)(2,1)} %blocks_h.1) | copy-start | bytes 11796484
  2.9 1.1 %copy-start.1 = (bf16[24,128,128]{2,1,0:T(8,128)(2,1)S(1)}, bf16[24,128,128]{2,1,0:T(8,128)(2,1)}, u32[]{:S(2)}) copy-start(bf16[24,128,128]{2,1,0:T(8,128)(2,1)} %precond_h.1) | copy-start | bytes 2359300
  4.0 0.9 %copy-start.2 = (f32[8,24,128]{2,1,0:T(8,128)S(1)}, f32[8,24,128]{2,1,0:T(8,128)}, u32[]{:S(2)}) copy-start(f32[8,24,128]{2,1,0:T(8,128)} %state_h.1) | copy-start | bytes 294916
  4.9 0.9 %copy-start.3 = (f32[8,24,128]{2,1,0:T(8,128)S(1)}, f32[8,24,128]{2,1,0:T(8,128)}, u32[]{:S(2)}) copy-start(f32[8,24,128]{2,1,0:T(8,128)} %forcing_h.1) | copy-start | bytes 294916
  5.8 0.9 %copy-start.4 = (f32[3,64,128]{2,1,0:T(8,128)S(1)}, f32[3,64,128]{2,1,0:T(8,128)}, u32[]{:S(2)}) copy-start(f32[3,64,128]{2,1,0:T(8,128)} %constant.2.clone.table_h) | copy-start | bytes 294916
  6.7 0.7 %copy-start.5 = (f32[24,128]{1,0:T(8,128)S(1)}, f32[24,128]{1,0:T(8,128)}, u32[]{:S(2)}) copy-start(f32[24,128]{1,0:T(8,128)} %initial_h.1) | copy-start | bytes 36868

commit v2 on v1

--- a/solution.py
+++ b/solution.py
@@ -200,12 +200,56 @@
     lam_own, lam_swap = columns(lam * coef)
     swap = np.roll(np.eye(steps), half, 1)
     inverse = inverse @ (np.diag(coef_own) + np.diag(coef_swap) @ swap)
-    factors = np.zeros((steps, steps))
     lanes = -(-steps // 128) * 128
+    factors = np.zeros((steps, lanes), np.float32)
     for place, column in enumerate((coef_own, coef_swap, lam_own, lam_swap)):
         factors[:, place] = column
-    stacked = np.stack([forward, inverse, factors])
-    return np.pad(stacked, ((0, 0), (0, 0), (0, lanes - steps))).astype(np.float32)
+    matrices = np.stack([np.tile(matrix, 2) for matrix in (forward, inverse)])
+    return matrices.astype(np.float32), factors
+
+
+def halves(field, axis):
+    high = field.astype(jnp.bfloat16)
+    low = (field - high.astype(jnp.float32)).astype(jnp.bfloat16)
+    return jnp.concatenate([high, low], axis)
+
+
+def transformed(matrix, field):
+    both = halves(field, 0)
+    return jnp.dot(
+        halves(matrix, 1),
+        jnp.concatenate([both, both], 0),
+        preferred_element_type=jnp.float32,
+    )
+
+
+def bits_of(number, count):
+    return [lax.rem(lax.div(number, 1 << i), 2) for i in range(count)]
+
+
+def number_of(bits):
+    return sum(bit * (1 << i) for i, bit in enumerate(bits))
+
+
+def flipped(position, mask, count):
+    bits = bits_of(position, count)
+    return position + sum((1 - 2 * bits[i]) * (1 << i) for i in range(count) if mask >> i & 1)
+
+
+def rank_at(position, s, count):
+    bits = bits_of(position, count)
+    for i in reversed(range(count - 1)):
+        bits[i] = lax.rem(bits[i] + bits[i + 1], 2)
+    rank = number_of(bits)
+    return rank + lax.rem(s, 2) * ((1 << count) - 1 - 2 * rank)
+
+
+def position_at(rank, s, count):
+    rank = rank + lax.rem(s, 2) * ((1 << count) - 1 - 2 * rank)
+    bits = bits_of(rank, count)
+    for i in range(count - 1):
+        bits[i] = lax.rem(bits[i] + bits[i + 1], 2)
+    return number_of(bits)
 
 
 def kernel(
@@ -216,14 +260,16 @@
     blocks_h,
     precond_h,
     couple_s,
-    table_h,
+    matrix_h,
+    factor_h,
     out_ref,
     state_v,
     forcing_v,
     initial_v,
     wb,
     wp,
-    table_v,
+    matrix_v,
+    factor_v,
     chunk,
     edge,
     diff,
@@ -251,17 +297,20 @@
     half = total // 2
     t = lax.axis_index("tm")
     s = lax.axis_index("space")
-    first, last = t == 0, t == nt - 1
+    level = nt.bit_length() - 1
+    rank = rank_at(t, s, level)
+    first, last = rank == 0, rank == nt - 1
+    targets = [flipped(t, o, level) for o in range(nt)]
+    ranks = [rank_at(target, s, level) for target in targets]
+    order = range(nt - 1, 0, -1)
     below, above = s > 0, s < ns - 1
     lower, upper = jnp.maximum(s - 1, 0), jnp.minimum(s + 1, ns - 1)
     low_edge = jnp.logical_and(first, below)
     high_edge = jnp.logical_and(last, above)
 
     barrier = pltpu.get_barrier_semaphore()
-    for o in range(1, nt):
-        pl.semaphore_signal(
-            barrier, inc=1, device_id=(lax.rem(t + o, nt), s), device_id_type=MESH
-        )
+    for o in order:
+        pl.semaphore_signal(barrier, inc=1, device_id=(targets[o], s), device_id_type=MESH)
 
     @pl.when(low_edge)
     def _():
@@ -273,7 +322,7 @@
         for o in range(nt):
             pl.semaphore_signal(barrier, inc=1, device_id=(o, upper), device_id_type=MESH)
 
-    start = t * own
+    start = rank * own
     loads = [
         pltpu.make_async_copy(source, target, local_sem.at[place])
         for place, (source, target) in enumerate(
@@ -282,7 +331,8 @@
                 (forcing_h, forcing_v),
                 (initial_h, initial_v),
                 (blocks_h.at[:, pl.ds(start, own)], wb),
-                (table_h, table_v),
+                (matrix_h, matrix_v),
+                (factor_h, factor_v),
                 (precond_h.at[pl.ds(start, own)], wp),
             )
         )
@@ -311,12 +361,37 @@
     signals = nt - 1 + jnp.where(below, 1, 0) + jnp.where(above, 1, 0)
     pl.semaphore_wait(barrier, signals)
 
+    edge_up = pltpu.make_async_remote_copy(
+        src_ref=edge.at[0],
+        dst_ref=redge.at[t],
+        send_sem=edge_send.at[0],
+        recv_sem=edge_recv.at[t],
+        device_id=(position_at(0, upper, level), upper),
+        device_id_type=MESH,
+    )
+    edge_down = pltpu.make_async_remote_copy(
+        src_ref=edge.at[1],
+        dst_ref=redge.at[t],
+        send_sem=edge_send.at[1],
+        recv_sem=edge_recv.at[t],
+        device_id=(position_at(nt - 1, lower, level), lower),
+        device_id_type=MESH,
+    )
+
+    @pl.when(above)
+    def _():
+        edge_up.start()
+
+    @pl.when(below)
+    def _():
+        edge_down.start()
+
     q_copies = []
-    for o in range(1, nt):
-        target = lax.rem(t + o, nt)
+    for o in order:
+        target = targets[o]
         q_copies.append(
             pltpu.make_async_remote_copy(
-                src_ref=chunk.at[target],
+                src_ref=chunk.at[ranks[o]],
                 dst_ref=rq.at[t],
                 send_sem=q_send.at[o],
                 recv_sem=q_recv.at[o],
@@ -326,43 +401,19 @@
         )
     for copy in q_copies:
         copy.start()
-    edge_up = pltpu.make_async_remote_copy(
-        src_ref=edge.at[0],
-        dst_ref=redge.at[t],
-        send_sem=edge_send.at[0],
-        recv_sem=edge_recv.at[t],
-        device_id=(0, upper),
-        device_id_type=MESH,
-    )
-    edge_down = pltpu.make_async_remote_copy(
-        src_ref=edge.at[1],
-        dst_ref=redge.at[t],
-        send_sem=edge_send.at[1],
-        recv_sem=edge_recv.at[t],
-        device_id=(nt - 1, lower),
-        device_id_type=MESH,
-    )
-
-    @pl.when(above)
-    def _():
-        edge_up.start()
-
-    @pl.when(below)
-    def _():
-        edge_down.start()
 
     loads[1].wait()
     loads[2].wait()
     forcing = forcing_v[...]
-    initial = jnp.where(first, initial_v[...], 0.0)
+    initial = jnp.where(t == 0, initial_v[...], 0.0)
     previous = jnp.concatenate([initial[None], state[:-1]], 0)
     diff[...] = jnp.swapaxes(forcing - state + previous, 0, 1)
     d_copies = []
-    for o in range(1, nt):
-        target = lax.rem(t + o, nt)
+    for o in order:
+        target = targets[o]
         d_copies.append(
             pltpu.make_async_remote_copy(
-                src_ref=diff.at[pl.ds(target * own, own)],
+                src_ref=diff.at[pl.ds(ranks[o] * own, own)],
                 dst_ref=rd.at[t],
                 send_sem=d_send.at[o],
                 recv_sem=d_recv.at[o],
@@ -372,7 +423,7 @@
         )
     for copy in d_copies:
         copy.start()
-    rq[t] = chunk[t]
+    rq[t] = chunk[rank]
     rd[t] = diff[pl.ds(start, own)]
 
     for copy in q_copies:
@@ -415,7 +466,7 @@
 
     def coupled(field, e):
         slots = wb.shape[0]
-        rows = [field[e + 2 + couple_s[start + e, slot]] for slot in range(slots)]
+        rows = [field[e + 2 + couple_s[slot, start + e]] for slot in range(slots)]
         weights = [wb[slot, e] for slot in range(slots)]
         return lax.dot_general(
             jnp.concatenate(rows, 1),
@@ -451,30 +502,30 @@
             parts.append(rd[source, e] + jnp.where(leading, carried, 0.0))
         residual.append(jnp.concatenate(parts, 0) - time_step * flux[e])
     loads[4].wait()
-    spectrum = jnp.dot(
-        table_v[0][:, :total],
-        jnp.concatenate(residual, 1),
-        precision=HIGHEST,
-        preferred_element_type=jnp.float32,
-    )
+    spectrum = transformed(matrix_v[0], jnp.concatenate(residual, 1))
 
     loads[5].wait()
+    loads[6].wait()
     first_step = conditioned(spectrum.astype(jnp.bfloat16))
     swapped = jnp.concatenate([first_step[half:], first_step[:half]], 0)
-    factors = table_v[2]
+    factors = factor_v[...]
     sol = factors[:, 0:1] * first_step + factors[:, 1:2] * swapped
     size = wp.shape[1]
     for e in range(own):
         xsol[2 + e] = sol[:, e * size : (e + 1) * size].astype(jnp.bfloat16)
 
-    has_down = jnp.logical_or(t > 0, below)
-    has_up = jnp.logical_or(t < nt - 1, above)
+    has_down = jnp.logical_or(rank > 0, below)
+    has_up = jnp.logical_or(rank < nt - 1, above)
+    down_s = jnp.where(first, lower, s)
+    down_t = position_at(jnp.where(first, nt - 1, rank - 1), down_s, level)
+    up_s = jnp.where(last, upper, s)
+    up_t = position_at(jnp.where(last, 0, rank + 1), up_s, level)
     halo_down = pltpu.make_async_remote_copy(
         src_ref=xsol.at[pl.ds(2, 2)],
         dst_ref=xsol.at[pl.ds(own + 2, 2)],
         send_sem=halo_send.at[0],
         recv_sem=halo_recv.at[0],
-        device_id=(jnp.where(first, nt - 1, t - 1), jnp.where(first, lower, s)),
+        device_id=(down_t, down_s),
         device_id_type=MESH,
     )
     halo_up = pltpu.make_async_remote_copy(
@@ -482,7 +533,7 @@
         dst_ref=xsol.at[pl.ds(0, 2)],
         send_sem=halo_send.at[1],
         recv_sem=halo_recv.at[1],
-        device_id=(jnp.where(last, 0, t + 1), jnp.where(last, upper, s)),
+        device_id=(up_t, up_s),
         device_id_type=MESH,
     )
 
@@ -515,14 +566,12 @@
     applied = jnp.concatenate([coupled(xsol, e) for e in range(own)], 1)
     left = left - time_step * applied
     steps_sum = first_step + conditioned(left.astype(jnp.bfloat16))
-    change = jnp.dot(
-        table_v[1][:, :total], steps_sum, precision=HIGHEST, preferred_element_type=jnp.float32
-    )
+    change = transformed(matrix_v[1], steps_sum)
     for e in range(own):
         back[e] = change[:, e * size : (e + 1) * size]
     b_copies = []
-    for o in range(1, nt):
-        target = lax.rem(t + o, nt)
+    for o in order:
+        target = targets[o]
         b_copies.append(
             pltpu.make_async_remote_copy(
                 src_ref=back.at[:, pl.ds(pl.multiple_of(target * steps, steps), steps)],
@@ -566,15 +615,15 @@
     own = width // nt
     total = nt * steps
     slots = blocks.shape[0]
-    table = jnp.asarray(tables(total))
-    anywhere = pl.BlockSpec(memory_space=pl.ANY)
+    matrix, factor = (jnp.asarray(table) for table in tables(total))
+    far = pl.BlockSpec(memory_space=pltpu.HBM)
     rows = (own + 5) * steps
     f32, b16 = jnp.float32, jnp.bfloat16
     dma = pltpu.SemaphoreType.DMA
     change = pl.pallas_call(
         functools.partial(kernel, (nt, ns, steps, width, own)),
         out_shape=jax.ShapeDtypeStruct(state.shape, f32),
-        in_specs=[anywhere] * 5 + [pl.BlockSpec(memory_space=pltpu.SMEM), anywhere],
+        in_specs=[far] * 5 + [pl.BlockSpec(memory_space=pltpu.SMEM)] + [far] * 2,
         out_specs=pl.BlockSpec(memory_space=pltpu.VMEM),
         scratch_shapes=[
             pltpu.VMEM(state.shape, f32),
@@ -582,7 +631,8 @@
             pltpu.VMEM(initial.shape, f32),
             pltpu.VMEM((slots, own, size, size), b16),
             pltpu.VMEM((own, size, size), b16),
-            pltpu.VMEM(table.shape, f32),
+            pltpu.VMEM(matrix.shape, f32),
+            pltpu.VMEM(factor.shape, f32),
             pltpu.VMEM((nt, rows, size), b16),
             pltpu.VMEM((2, 2 * steps, size), b16),
             pltpu.VMEM((width, steps, size), f32),
@@ -593,7 +643,7 @@
             pltpu.VMEM((own + 4, total, size), b16),
             pltpu.VMEM((own, total, size), f32),
             pltpu.VMEM((width, steps, size), f32),
-            dma((6,)),
+            dma((7,)),
             dma((nt,)),
             dma((nt,)),
             dma((nt,)),
@@ -606,9 +656,9 @@
             dma((nt,)),
         ],
         compiler_params=pltpu.CompilerParams(
-            collective_id=0, has_side_effects=True, vmem_limit_bytes=24 * 1024 * 1024
+            collective_id=0, has_side_effects=True, vmem_limit_bytes=60 * 1024 * 1024
         ),
-    )(state, forcing, initial, blocks, precond, couple, table)
+    )(state, forcing, initial, blocks, precond, couple.T, matrix, factor)
     return state + change
 
 
@@ -617,7 +667,8 @@
     steps, width, _ = state.shape
     own = width // nt
     even_cut = width % nt == 0 and own >= 2 and 2 * own <= steps and steps % 8 == 0
-    if nt > 1 and even_cut and (own + 5) * steps % 16 == 0:
+    power = nt > 1 and nt & nt - 1 == 0 and nt * steps % 16 == 0
+    if power and even_cut and (own + 5) * steps % 16 == 0:
         return on_device_blocks(state, forcing, initial, blocks, precond, couple)
     return on_device_steps(state, forcing, initial, blocks, precond, couple)
 

time: 26.2 us -> 20 us (0.76)
  local copies, waits for them, and re-layouts: 7.39 us -> 0.01 us
  other arithmetic: 0.66 us -> 1.55 us
  Pallas kernels: 17.7 us -> 18.2 us
    unnamed x13 -> x2, local copies, waits for them, and re-layouts: 7.39 us -> 0.01 us
    add x1, other arithmetic: 0.66 us -> 1.55 us  [on_device_blocks(): return state + change]
    pallas_call x1, Pallas kernels: 17.7 us -> 18.2 us  [on_device_blocks(): pl.pallas_call(functools.partial(kernel, (nt, ns, steps, width, own)), ou...]
where the time goes in v2:
time: 20 us; the launch traced here: 19.8 us
  Pallas kernels  18.2 us (91%)
  other arithmetic  1.55 us (8%)
    pallas_call x1, Pallas kernels, on_device_blocks(): pl.pallas_call(functools.partial(kernel, (nt, ns, steps, width, own)), ou...  18.2 us
    add x1, other arithmetic, on_device_blocks(): return state + change  1.55 us

profile of v2, /device:TPU:0, one launch (start us, length us, event | category | flops | bytes accessed | tf_op | source)
XLA Modules:
  0.0 19.8 jit_solution(16753006352429139242)
XLA Ops:
  0.0 0.0 copy-start
  0.0 18.2 %shard_map.82 = f32[8,24,128]{2,1,0:T(8,128)} custom-call(f32[8,24,128]{2,1,0:T(8,128)} %state_h.1, f32[8,24,128]{2,1,0:T(8,128)} %forcing_h.1, f32[24,128]{1,0:T(8,128)} %initial_h.1, bf16[5,24,128,128]{3,2,1,0:T(8,128)(2,1)} %blocks_h.1, bf16[24,128,128]{2,1,0:T(8,128)(2,1)} %precond_h.1, s32[5,24]{1,0:T(8,128)} %bitcast.1, ...), custom_call_target="tpu_custom_call" | custom-call | tf_op jit(solution)/shard_map/pallas_call | solution.py:623
  18.2 0.0 copy-done
  18.3 1.5 %add.3 = f32[8,24,128]{2,1,0:T(8,128)} add(f32[8,24,128]{2,1,0:T(8,128)S(1)} %copy-done, f32[8,24,128]{2,1,0:T(8,128)} %shard_map.82) | non-fusion elementwise | flops 24576 | bytes 294912 | tf_op jit(solution)/shard_map/add | solution.py:662
Async XLA Ops:
  0.0 18.2 %copy-start = (f32[8,24,128]{2,1,0:T(8,128)S(1)}, f32[8,24,128]{2,1,0:T(8,128)}, u32[]{:S(2)}) copy-start(f32[8,24,128]{2,1,0:T(8,128)} %state_h.1) | copy-start | bytes 294916

commit v3 on v2

--- a/solution.py
+++ b/solution.py
@@ -231,24 +231,25 @@
     return sum(bit * (1 << i) for i, bit in enumerate(bits))
 
 
-def flipped(position, mask, count):
-    bits = bits_of(position, count)
-    return position + sum((1 - 2 * bits[i]) * (1 << i) for i in range(count) if mask >> i & 1)
-
-
-def rank_at(position, s, count):
-    bits = bits_of(position, count)
-    for i in reversed(range(count - 1)):
-        bits[i] = lax.rem(bits[i] + bits[i + 1], 2)
-    rank = number_of(bits)
-    return rank + lax.rem(s, 2) * ((1 << count) - 1 - 2 * rank)
-
-
-def position_at(rank, s, count):
-    rank = rank + lax.rem(s, 2) * ((1 << count) - 1 - 2 * rank)
-    bits = bits_of(rank, count)
+def flipped(bits, mask):
+    return [1 - bit if mask >> i & 1 else bit for i, bit in enumerate(bits)]
+
+
+def differ(a, b):
+    return a + b - 2 * a * b
+
+
+def rank_at(bits, odd):
+    bits = list(bits)
+    for i in reversed(range(len(bits) - 1)):
+        bits[i] = differ(bits[i], bits[i + 1])
+    return number_of([differ(bit, odd) for bit in bits])
+
+
+def position_at(rank, odd, count):
+    bits = [differ(bit, odd) for bit in bits_of(rank, count)]
     for i in range(count - 1):
-        bits[i] = lax.rem(bits[i] + bits[i + 1], 2)
+        bits[i] = differ(bits[i], bits[i + 1])
     return number_of(bits)
 
 
@@ -259,7 +260,7 @@
     initial_h,
     blocks_h,
     precond_h,
-    couple_s,
+    couple_h,
     matrix_h,
     factor_h,
     out_ref,
@@ -270,6 +271,7 @@
     wp,
     matrix_v,
     factor_v,
+    couple_s,
     chunk,
     edge,
     diff,
@@ -298,11 +300,16 @@
     t = lax.axis_index("tm")
     s = lax.axis_index("space")
     level = nt.bit_length() - 1
-    rank = rank_at(t, s, level)
+    odd = lax.rem(s, 2)
+    place_bits = bits_of(t, level)
+    rank = rank_at(place_bits, odd)
     first, last = rank == 0, rank == nt - 1
-    targets = [flipped(t, o, level) for o in range(nt)]
-    ranks = [rank_at(target, s, level) for target in targets]
+    targets = [number_of(flipped(place_bits, o)) for o in range(nt)]
+    ranks = [rank_at(flipped(place_bits, o), odd) for o in range(nt)]
     order = range(nt - 1, 0, -1)
+    top = nt // 2
+    first_place = odd * top, (1 - odd) * top
+    last_place = first_place[1], first_place[0]
     below, above = s > 0, s < ns - 1
     lower, upper = jnp.maximum(s - 1, 0), jnp.minimum(s + 1, ns - 1)
     low_edge = jnp.logical_and(first, below)
@@ -334,6 +341,7 @@
                 (matrix_h, matrix_v),
                 (factor_h, factor_v),
                 (precond_h.at[pl.ds(start, own)], wp),
+                (couple_h, couple_s),
             )
         )
     ]
@@ -366,7 +374,7 @@
         dst_ref=redge.at[t],
         send_sem=edge_send.at[0],
         recv_sem=edge_recv.at[t],
-        device_id=(position_at(0, upper, level), upper),
+        device_id=(first_place[1], upper),
         device_id_type=MESH,
     )
     edge_down = pltpu.make_async_remote_copy(
@@ -374,7 +382,7 @@
         dst_ref=redge.at[t],
         send_sem=edge_send.at[1],
         recv_sem=edge_recv.at[t],
-        device_id=(position_at(nt - 1, lower, level), lower),
+        device_id=(last_place[1], lower),
         device_id_type=MESH,
     )
 
@@ -463,6 +471,7 @@
         take_edge(own + 2)
 
     loads[3].wait()
+    loads[7].wait()
 
     def coupled(field, e):
         slots = wb.shape[0]
@@ -517,9 +526,11 @@
     has_down = jnp.logical_or(rank > 0, below)
     has_up = jnp.logical_or(rank < nt - 1, above)
     down_s = jnp.where(first, lower, s)
-    down_t = position_at(jnp.where(first, nt - 1, rank - 1), down_s, level)
+    before = position_at(jnp.maximum(rank - 1, 0), odd, level)
+    down_t = jnp.where(first, last_place[1], before)
     up_s = jnp.where(last, upper, s)
-    up_t = position_at(jnp.where(last, 0, rank + 1), up_s, level)
+    after = position_at(jnp.minimum(rank + 1, nt - 1), odd, level)
+    up_t = jnp.where(last, first_place[1], after)
     halo_down = pltpu.make_async_remote_copy(
         src_ref=xsol.at[pl.ds(2, 2)],
         dst_ref=xsol.at[pl.ds(own + 2, 2)],
@@ -587,7 +598,7 @@
     rback[pl.ds(start, own)] = back[:, pl.ds(pl.multiple_of(t * steps, steps), steps)]
     for copy in b_copies:
         copy.wait_recv()
-    out_ref[...] = jnp.swapaxes(rback[...], 0, 1)
+    out_ref[...] = state_v[...] + jnp.swapaxes(rback[...], 0, 1)
 
     for copy in q_copies + d_copies + b_copies:
         copy.wait_send()
@@ -620,10 +631,10 @@
     rows = (own + 5) * steps
     f32, b16 = jnp.float32, jnp.bfloat16
     dma = pltpu.SemaphoreType.DMA
-    change = pl.pallas_call(
+    return pl.pallas_call(
         functools.partial(kernel, (nt, ns, steps, width, own)),
         out_shape=jax.ShapeDtypeStruct(state.shape, f32),
-        in_specs=[far] * 5 + [pl.BlockSpec(memory_space=pltpu.SMEM)] + [far] * 2,
+        in_specs=[far] * 8,
         out_specs=pl.BlockSpec(memory_space=pltpu.VMEM),
         scratch_shapes=[
             pltpu.VMEM(state.shape, f32),
@@ -633,6 +644,7 @@
             pltpu.VMEM((own, size, size), b16),
             pltpu.VMEM(matrix.shape, f32),
             pltpu.VMEM(factor.shape, f32),
+            pltpu.SMEM(couple.shape[::-1], jnp.int32),
             pltpu.VMEM((nt, rows, size), b16),
             pltpu.VMEM((2, 2 * steps, size), b16),
             pltpu.VMEM((width, steps, size), f32),
@@ -643,7 +655,7 @@
             pltpu.VMEM((own + 4, total, size), b16),
             pltpu.VMEM((own, total, size), f32),
             pltpu.VMEM((width, steps, size), f32),
-            dma((7,)),
+            dma((8,)),
             dma((nt,)),
             dma((nt,)),
             dma((nt,)),
@@ -659,7 +671,6 @@
             collective_id=0, has_side_effects=True, vmem_limit_bytes=60 * 1024 * 1024
         ),
     )(state, forcing, initial, blocks, precond, couple.T, matrix, factor)
-    return state + change
 
 
 def on_device(state, forcing, initial, blocks, precond, couple):

time: 20 us -> 18.9 us (0.945)
  other arithmetic: 1.55 us -> 0 us
  local copies, waits for them, and re-layouts: 0.01 us -> 1.54 us
  Pallas kernels: 18.2 us -> 17.2 us
    add x1 -> x0, other arithmetic: 1.55 us -> none  [on_device_blocks(): return state + change]
    unnamed x2 -> x1, local copies, waits for them, and re-layouts: 0.01 us -> 1.54 us
    pallas_call x1, Pallas kernels: 18.2 us -> 17.2 us  [on_device_blocks(): pl.pallas_call(functools.partial(kernel, (nt, ns, steps, width, own)), ou...]
where the time goes in v3:
time: 18.9 us; the launch traced here: 18.7 us
  Pallas kernels  17.2 us (91%)
  local copies, waits for them, and re-layouts  1.54 us (8%)
    pallas_call x1, Pallas kernels, on_device_blocks(): pl.pallas_call(functools.partial(kernel, (nt, ns, steps, width, own)), ou...  17.2 us
    unnamed x1, local copies, waits for them, and re-layouts  1.54 us

profile of v3, /device:TPU:0, one launch (start us, length us, event | category | flops | bytes accessed | tf_op | source)
XLA Modules:
  0.0 18.7 jit_solution(2602892955354340310)
XLA Ops:
  0.0 17.2 %shard_map.82 = f32[8,24,128]{2,1,0:T(8,128)} custom-call(f32[8,24,128]{2,1,0:T(8,128)} %state_h.1, f32[8,24,128]{2,1,0:T(8,128)} %forcing_h.1, f32[24,128]{1,0:T(8,128)} %initial_h.1, bf16[5,24,128,128]{3,2,1,0:T(8,128)(2,1)} %blocks_h.1, bf16[24,128,128]{2,1,0:T(8,128)(2,1)} %precond_h.1, s32[5,24]{1,0:T(8,128)} %bitcast.1, ...), custom_call_target="tpu_custom_call" | custom-call | tf_op jit(solution)/shard_map/pallas_call | solution.py:634
  17.2 1.5 %copy.10 = f32[8,24,128]{2,1,0:T(8,128)} copy(f32[8,24,128]{2,1,0:T(8,128)} %shard_map.82) | data formatting | bytes 196608

commit v4 on v3

--- a/solution.py
+++ b/solution.py
@@ -633,7 +633,7 @@
     dma = pltpu.SemaphoreType.DMA
     return pl.pallas_call(
         functools.partial(kernel, (nt, ns, steps, width, own)),
-        out_shape=jax.ShapeDtypeStruct(state.shape, f32),
+        out_shape=pltpu.VMEM(state.shape, f32),
         in_specs=[far] * 8,
         out_specs=pl.BlockSpec(memory_space=pltpu.VMEM),
         scratch_shapes=[

time: 18.9 us -> 17.4 us (0.921)
  local copies, waits for them, and re-layouts: 1.54 us -> 0.64 us
  Pallas kernels: 17.2 us -> 16.6 us
    unnamed x1, local copies, waits for them, and re-layouts: 1.54 us -> 0.64 us
    pallas_call x1, Pallas kernels: 17.2 us -> 16.6 us  [on_device_blocks(): pl.pallas_call(functools.partial(kernel, (nt, ns, steps, width, own)), ou...]
where the time goes in v4:
time: 17.4 us; the launch traced here: 17.2 us
  Pallas kernels  16.6 us (95%)
  local copies, waits for them, and re-layouts  0.64 us (4%)
    pallas_call x1, Pallas kernels, on_device_blocks(): pl.pallas_call(functools.partial(kernel, (nt, ns, steps, width, own)), ou...  16.6 us
    unnamed x1, local copies, waits for them, and re-layouts  0.64 us

profile of v4, /device:TPU:0, one launch (start us, length us, event | category | flops | bytes accessed | tf_op | source)
XLA Modules:
  0.0 17.2 jit_solution(6992657461437066884)
XLA Ops:
  0.0 16.6 %shard_map.82 = f32[8,24,128]{2,1,0:T(8,128)S(1)} custom-call(f32[8,24,128]{2,1,0:T(8,128)} %state_h.1, f32[8,24,128]{2,1,0:T(8,128)} %forcing_h.1, f32[24,128]{1,0:T(8,128)} %initial_h.1, bf16[5,24,128,128]{3,2,1,0:T(8,128)(2,1)} %blocks_h.1, bf16[24,128,128]{2,1,0:T(8,128)(2,1)} %precond_h.1, s32[5,24]{1,0:T(8,128)} %bitcast.1, ...), custom_call_target="tpu_custom_call" | custom-call | tf_op jit(solution)/shard_map/pallas_call | solution.py:634
  16.6 0.6 %copy.10 = f32[8,24,128]{2,1,0:T(8,128)} copy(f32[8,24,128]{2,1,0:T(8,128)S(1)} %shard_map.82) | data formatting | bytes 196608

commit v5 on v4

--- a/solution.py
+++ b/solution.py
@@ -170,8 +170,6 @@
 
 
 MESH = pl.DeviceIdType.MESH
-NT_DIMS = (((1,), (1,)), ((), ()))
-HIGHEST = lax.Precision.HIGHEST
 
 
 def tables(steps):
@@ -269,6 +267,8 @@
     initial_v,
     wb,
     wp,
+    wbt,
+    wpt,
     matrix_v,
     factor_v,
     couple_s,
@@ -315,20 +315,6 @@
     low_edge = jnp.logical_and(first, below)
     high_edge = jnp.logical_and(last, above)
 
-    barrier = pltpu.get_barrier_semaphore()
-    for o in order:
-        pl.semaphore_signal(barrier, inc=1, device_id=(targets[o], s), device_id_type=MESH)
-
-    @pl.when(low_edge)
-    def _():
-        for o in range(nt):
-            pl.semaphore_signal(barrier, inc=1, device_id=(o, lower), device_id_type=MESH)
-
-    @pl.when(high_edge)
-    def _():
-        for o in range(nt):
-            pl.semaphore_signal(barrier, inc=1, device_id=(o, upper), device_id_type=MESH)
-
     start = rank * own
     loads = [
         pltpu.make_async_copy(source, target, local_sem.at[place])
@@ -345,7 +331,24 @@
             )
         )
     ]
-    for load in loads:
+    for load in loads[:3]:
+        load.start()
+
+    barrier = pltpu.get_barrier_semaphore()
+    for o in order:
+        pl.semaphore_signal(barrier, inc=1, device_id=(targets[o], s), device_id_type=MESH)
+
+    @pl.when(low_edge)
+    def _():
+        for o in range(nt):
+            pl.semaphore_signal(barrier, inc=1, device_id=(o, lower), device_id_type=MESH)
+
+    @pl.when(high_edge)
+    def _():
+        for o in range(nt):
+            pl.semaphore_signal(barrier, inc=1, device_id=(o, upper), device_id_type=MESH)
+
+    for load in loads[3:]:
         load.start()
 
     loads[0].wait()
@@ -434,6 +437,15 @@
     rq[t] = chunk[rank]
     rd[t] = diff[pl.ds(start, own)]
 
+    loads[3].wait()
+    slots, size = wb.shape[0], wb.shape[2]
+    for e in range(own):
+        for slot in range(slots):
+            wbt[e, slot * size : (slot + 1) * size] = wb[slot, e].T
+    loads[6].wait()
+    for e in range(own):
+        wpt[e] = wp[e].T
+
     for copy in q_copies:
         copy.wait_recv()
     got = [rq[source].astype(jnp.float32) for source in range(nt)]
@@ -470,28 +482,20 @@
     def _():
         take_edge(own + 2)
 
-    loads[3].wait()
     loads[7].wait()
 
     def coupled(field, e):
-        slots = wb.shape[0]
         rows = [field[e + 2 + couple_s[slot, start + e]] for slot in range(slots)]
-        weights = [wb[slot, e] for slot in range(slots)]
-        return lax.dot_general(
-            jnp.concatenate(rows, 1),
-            jnp.concatenate(weights, 1),
-            NT_DIMS,
-            preferred_element_type=jnp.float32,
+        return jnp.dot(
+            jnp.concatenate(rows, 1), wbt[e], preferred_element_type=jnp.float32
         )
 
     def conditioned(rounded):
-        size = wp.shape[1]
         return jnp.concatenate(
             [
-                lax.dot_general(
+                jnp.dot(
                     rounded[:, e * size : (e + 1) * size],
-                    wp[e],
-                    NT_DIMS,
+                    wpt[e],
                     preferred_element_type=jnp.float32,
                 )
                 for e in range(own)
@@ -514,12 +518,10 @@
     spectrum = transformed(matrix_v[0], jnp.concatenate(residual, 1))
 
     loads[5].wait()
-    loads[6].wait()
     first_step = conditioned(spectrum.astype(jnp.bfloat16))
     swapped = jnp.concatenate([first_step[half:], first_step[:half]], 0)
     factors = factor_v[...]
     sol = factors[:, 0:1] * first_step + factors[:, 1:2] * swapped
-    size = wp.shape[1]
     for e in range(own):
         xsol[2 + e] = sol[:, e * size : (e + 1) * size].astype(jnp.bfloat16)
 
@@ -641,6 +643,8 @@
             pltpu.VMEM(state.shape, f32),
             pltpu.VMEM(initial.shape, f32),
             pltpu.VMEM((slots, own, size, size), b16),
+            pltpu.VMEM((own, size, size), b16),
+            pltpu.VMEM((own, slots * size, size), b16),
             pltpu.VMEM((own, size, size), b16),
             pltpu.VMEM(matrix.shape, f32),
             pltpu.VMEM(factor.shape, f32),

time: 17.4 us -> 17.2 us (0.989)
  Pallas kernels: 16.6 us -> 16.4 us
where the time goes in v5:
time: 17.2 us; the launch traced here: 17.1 us
  Pallas kernels  16.4 us (95%)
  local copies, waits for them, and re-layouts  0.64 us (4%)
    pallas_call x1, Pallas kernels, on_device_blocks(): pl.pallas_call(functools.partial(kernel, (nt, ns, steps, width, own)), ou...  16.4 us
    unnamed x1, local copies, waits for them, and re-layouts  0.64 us

profile of v5, /device:TPU:0, one launch (start us, length us, event | category | flops | bytes accessed | tf_op | source)
XLA Modules:
  0.0 17.1 jit_solution(1087463540674146589)
XLA Ops:
  0.0 16.4 %shard_map.82 = f32[8,24,128]{2,1,0:T(8,128)S(1)} custom-call(f32[8,24,128]{2,1,0:T(8,128)} %state_h.1, f32[8,24,128]{2,1,0:T(8,128)} %forcing_h.1, f32[24,128]{1,0:T(8,128)} %initial_h.1, bf16[5,24,128,128]{3,2,1,0:T(8,128)(2,1)} %blocks_h.1, bf16[24,128,128]{2,1,0:T(8,128)(2,1)} %precond_h.1, s32[5,24]{1,0:T(8,128)} %bitcast.1, ...), custom_call_target="tpu_custom_call" | custom-call | tf_op jit(solution)/shard_map/pallas_call | solution.py:636
  16.5 0.6 %copy.10 = f32[8,24,128]{2,1,0:T(8,128)} copy(f32[8,24,128]{2,1,0:T(8,128)S(1)} %shard_map.82) | data formatting | bytes 196608

commit v6 on v5

--- a/solution.py
+++ b/solution.py
@@ -306,7 +306,7 @@
     first, last = rank == 0, rank == nt - 1
     targets = [number_of(flipped(place_bits, o)) for o in range(nt)]
     ranks = [rank_at(flipped(place_bits, o), odd) for o in range(nt)]
-    order = range(nt - 1, 0, -1)
+    order = sorted(range(1, nt), key=lambda o: (o < 2, -(o % 2), -o))
     top = nt // 2
     first_place = odd * top, (1 - odd) * top
     last_place = first_place[1], first_place[0]
@@ -598,28 +598,30 @@
     for copy in b_copies:
         copy.start()
     rback[pl.ds(start, own)] = back[:, pl.ds(pl.multiple_of(t * steps, steps), steps)]
+    for copy in q_copies + d_copies:
+        copy.wait_send()
+
+    @pl.when(above)
+    def _():
+        edge_up.wait_send()
+
+    @pl.when(below)
+    def _():
+        edge_down.wait_send()
+
+    @pl.when(has_down)
+    def _():
+        halo_down.wait_send()
+
+    @pl.when(has_up)
+    def _():
+        halo_up.wait_send()
+
+    for copy in b_copies:
+        copy.wait_send()
     for copy in b_copies:
         copy.wait_recv()
     out_ref[...] = state_v[...] + jnp.swapaxes(rback[...], 0, 1)
-
-    for copy in q_copies + d_copies + b_copies:
-        copy.wait_send()
-
-    @pl.when(above)
-    def _():
-        edge_up.wait_send()
-
-    @pl.when(below)
-    def _():
-        edge_down.wait_send()
-
-    @pl.when(has_down)
-    def _():
-        halo_down.wait_send()
-
-    @pl.when(has_up)
-    def _():
-        halo_up.wait_send()
 
 
 def on_device_blocks(state, forcing, initial, blocks, precond, couple):

time: 17.2 us -> 17.3 us (level)
  no operation moved by 1% of the time
where the time goes in v6:
time: 17.3 us; the launch traced here: 17.1 us
  Pallas kernels  16.5 us (95%)
  local copies, waits for them, and re-layouts  0.64 us (4%)
    pallas_call x1, Pallas kernels, on_device_blocks(): pl.pallas_call(functools.partial(kernel, (nt, ns, steps, width, own)), ou...  16.5 us
    unnamed x1, local copies, waits for them, and re-layouts  0.64 us

profile of v6, /device:TPU:0, one launch (start us, length us, event | category | flops | bytes accessed | tf_op | source)
XLA Modules:
  0.0 17.1 jit_solution(11464682198270723836)
XLA Ops:
  0.0 16.5 %shard_map.82 = f32[8,24,128]{2,1,0:T(8,128)S(1)} custom-call(f32[8,24,128]{2,1,0:T(8,128)} %state_h.1, f32[8,24,128]{2,1,0:T(8,128)} %forcing_h.1, f32[24,128]{1,0:T(8,128)} %initial_h.1, bf16[5,24,128,128]{3,2,1,0:T(8,128)(2,1)} %blocks_h.1, bf16[24,128,128]{2,1,0:T(8,128)(2,1)} %precond_h.1, s32[5,24]{1,0:T(8,128)} %bitcast.1, ...), custom_call_target="tpu_custom_call" | custom-call | tf_op jit(solution)/shard_map/pallas_call | solution.py:638
  16.5 0.6 %copy.10 = f32[8,24,128]{2,1,0:T(8,128)} copy(f32[8,24,128]{2,1,0:T(8,128)S(1)} %shard_map.82) | data formatting | bytes 196608

commit v7 on v6

--- a/solution.py
+++ b/solution.py
@@ -352,15 +352,17 @@
         load.start()
 
     loads[0].wait()
-    state = state_v[...]
-    by_block = jnp.swapaxes(state, 0, 1)
-    squares = 0.5 * by_block * by_block
-    blank = jnp.zeros((steps, squares.shape[2]), jnp.float32)
+    squares = []
+    for j in range(width):
+        block = state_v[pl.ds(j, steps, stride=width)]
+        squares.append(0.5 * block * block)
+    blank = jnp.zeros((steps, state_v.shape[1]), jnp.float32)
+    final = state_v[(steps - 1) * width :]
     for target in range(nt):
         parts = []
         for j in range(own * target - 2, own * (target + 1) + 2):
             parts.append(squares[j] if 0 <= j < width else blank)
-        tail = state[steps - 1, own * target : own * (target + 1)]
+        tail = final[own * target : own * (target + 1)]
         tail_hi = tail.astype(jnp.bfloat16).astype(jnp.float32)
         parts += [tail_hi, tail - tail_hi]
         if steps > 2 * own:
@@ -415,10 +417,12 @@
 
     loads[1].wait()
     loads[2].wait()
-    forcing = forcing_v[...]
     initial = jnp.where(t == 0, initial_v[...], 0.0)
-    previous = jnp.concatenate([initial[None], state[:-1]], 0)
-    diff[...] = jnp.swapaxes(forcing - state + previous, 0, 1)
+    state = state_v[...]
+    previous = jnp.concatenate([initial, state[:-width]], 0)
+    forcing_v[...] = forcing_v[...] - state + previous
+    for j in range(width):
+        diff[j] = forcing_v[pl.ds(j, steps, stride=width)]
     d_copies = []
     for o in order:
         target = targets[o]
@@ -621,7 +625,9 @@
         copy.wait_send()
     for copy in b_copies:
         copy.wait_recv()
-    out_ref[...] = state_v[...] + jnp.swapaxes(rback[...], 0, 1)
+    for j in range(width):
+        rows = pl.ds(j, steps, stride=width)
+        out_ref[rows] = state_v[rows] + rback[j]
 
 
 def on_device_blocks(state, forcing, initial, blocks, precond, couple):
@@ -635,14 +641,15 @@
     rows = (own + 5) * steps
     f32, b16 = jnp.float32, jnp.bfloat16
     dma = pltpu.SemaphoreType.DMA
-    return pl.pallas_call(
+    flat = steps * width, size
+    corrected = pl.pallas_call(
         functools.partial(kernel, (nt, ns, steps, width, own)),
-        out_shape=pltpu.VMEM(state.shape, f32),
+        out_shape=pltpu.VMEM(flat, f32),
         in_specs=[far] * 8,
         out_specs=pl.BlockSpec(memory_space=pltpu.VMEM),
         scratch_shapes=[
-            pltpu.VMEM(state.shape, f32),
-            pltpu.VMEM(state.shape, f32),
+            pltpu.VMEM(flat, f32),
+            pltpu.VMEM(flat, f32),
             pltpu.VMEM(initial.shape, f32),
             pltpu.VMEM((slots, own, size, size), b16),
             pltpu.VMEM((own, size, size), b16),
@@ -676,7 +683,17 @@
         compiler_params=pltpu.CompilerParams(
             collective_id=0, has_side_effects=True, vmem_limit_bytes=60 * 1024 * 1024
         ),
-    )(state, forcing, initial, blocks, precond, couple.T, matrix, factor)
+    )(
+        state.reshape(flat),
+        forcing.reshape(flat),
+        initial,
+        blocks,
+        precond,
+        couple.T,
+        matrix,
+        factor,
+    )
+    return corrected.reshape(state.shape)
 
 
 def on_device(state, forcing, initial, blocks, precond, couple):

time: 17.3 us -> 17.3 us (level)
  no operation moved by 1% of the time
where the time goes in v7:
time: 17.3 us; the launch traced here: 17.1 us
  Pallas kernels  16.5 us (95%)
  local copies, waits for them, and re-layouts  0.64 us (4%)
    pallas_call x1, Pallas kernels, on_device_blocks(): pl.pallas_call(functools.partial(kernel, (nt, ns, steps, width, own)), ou...  16.5 us
    unnamed x1, local copies, waits for them, and re-layouts  0.64 us

profile of v7, /device:TPU:0, one launch (start us, length us, event | category | flops | bytes accessed | tf_op | source)
XLA Modules:
  0.0 17.1 jit_solution(2383503666782947543)
XLA Ops:
  0.0 16.5 %shard_map.82 = f32[192,128]{1,0:T(8,128)S(1)} custom-call(f32[192,128]{1,0:T(8,128)} %bitcast.5, f32[192,128]{1,0:T(8,128)} %bitcast.6, f32[24,128]{1,0:T(8,128)} %initial_h.1, bf16[5,24,128,128]{3,2,1,0:T(8,128)(2,1)} %blocks_h.1, bf16[24,128,128]{2,1,0:T(8,128)(2,1)} %precond_h.1, s32[5,24]{1,0:T(8,128)} %bitcast.7, ...), custom_call_target="tpu_custom_call" | custom-call | tf_op jit(solution)/shard_map/pallas_call | solution.py:645
  16.5 0.6 %copy.10 = f32[8,24,128]{2,1,0:T(8,128)} copy(f32[8,24,128]{2,1,0:T(8,128)S(1)} %bitcast.4) | data formatting | bytes 196608

commit v8 on v7

--- a/solution.py
+++ b/solution.py
@@ -582,25 +582,24 @@
 
     applied = jnp.concatenate([coupled(xsol, e) for e in range(own)], 1)
     left = left - time_step * applied
-    steps_sum = first_step + conditioned(left.astype(jnp.bfloat16))
-    change = transformed(matrix_v[1], steps_sum)
+    rounded = left.astype(jnp.bfloat16)
+    b_copies = []
     for e in range(own):
-        back[e] = change[:, e * size : (e + 1) * size]
-    b_copies = []
-    for o in order:
-        target = targets[o]
-        b_copies.append(
-            pltpu.make_async_remote_copy(
-                src_ref=back.at[:, pl.ds(pl.multiple_of(target * steps, steps), steps)],
-                dst_ref=rback.at[pl.ds(start, own)],
-                send_sem=b_send.at[o],
-                recv_sem=b_recv.at[o],
-                device_id=(target, s),
+        columns = slice(e * size, (e + 1) * size)
+        second_step = jnp.dot(rounded[:, columns], wpt[e], preferred_element_type=jnp.float32)
+        back[e] = transformed(matrix_v[1], first_step[:, columns] + second_step)
+        for o in order:
+            piece = pl.ds(pl.multiple_of(targets[o] * steps, steps), steps)
+            copy = pltpu.make_async_remote_copy(
+                src_ref=back.at[e, piece],
+                dst_ref=rback.at[start + e],
+                send_sem=b_send.at[e, o],
+                recv_sem=b_recv.at[e, o],
+                device_id=(targets[o], s),
                 device_id_type=MESH,
             )
-        )
-    for copy in b_copies:
-        copy.start()
+            copy.start()
+            b_copies.append(copy)
     rback[pl.ds(start, own)] = back[:, pl.ds(pl.multiple_of(t * steps, steps), steps)]
     for copy in q_copies + d_copies:
         copy.wait_send()
@@ -677,8 +676,8 @@
             dma((nt,)),
             dma((2,)),
             dma((2,)),
-            dma((nt,)),
-            dma((nt,)),
+            dma((own, nt)),
+            dma((own, nt)),
         ],
         compiler_params=pltpu.CompilerParams(
             collective_id=0, has_side_effects=True, vmem_limit_bytes=60 * 1024 * 1024

time: 17.3 us -> 17.8 us (1.029)
  Pallas kernels: 16.5 us -> 17 us
    pallas_call x1, Pallas kernels: 16.5 us -> 17 us  [on_device_blocks(): pl.pallas_call(functools.partial(kernel, (nt, ns, steps, width, own)), ou...]
where the time goes in v8:
time: 17.8 us; the launch traced here: 17.7 us
  Pallas kernels  17 us (96%)
  local copies, waits for them, and re-layouts  0.64 us (4%)
    pallas_call x1, Pallas kernels, on_device_blocks(): pl.pallas_call(functools.partial(kernel, (nt, ns, steps, width, own)), ou...  17 us
    unnamed x1, local copies, waits for them, and re-layouts  0.64 us

profile of v8, /device:TPU:0, one launch (start us, length us, event | category | flops | bytes accessed | tf_op | source)
XLA Modules:
  0.0 17.7 jit_solution(6734354481911888954)
XLA Ops:
  0.0 17.0 %shard_map.82 = f32[192,128]{1,0:T(8,128)S(1)} custom-call(f32[192,128]{1,0:T(8,128)} %bitcast.5, f32[192,128]{1,0:T(8,128)} %bitcast.6, f32[24,128]{1,0:T(8,128)} %initial_h.1, bf16[5,24,128,128]{3,2,1,0:T(8,128)(2,1)} %blocks_h.1, bf16[24,128,128]{2,1,0:T(8,128)(2,1)} %precond_h.1, s32[5,24]{1,0:T(8,128)} %bitcast.7, ...), custom_call_target="tpu_custom_call" | custom-call | tf_op jit(solution)/shard_map/pallas_call | solution.py:644
  17.0 0.6 %copy.10 = f32[8,24,128]{2,1,0:T(8,128)} copy(f32[8,24,128]{2,1,0:T(8,128)S(1)} %bitcast.4) | data formatting | bytes 196608
